TPU v7x, 32 devices: a whole 2x2x4 slice. The times are simulated.
32 devices in a mesh: rows: 4 (over x, core), cols: 8 (over z, y).
Axes of the slice: x: 2, y: 2, z: 4, core: 2. Of those that a mesh axis runs over, the one named last changes fastest.
Arguments:
- upper: float32 [4096, 4096], P(('rows', 'cols')), as said below
- matching: int32 [2, 16], replicated, may hold values from 0 to 15, as said below
Outputs:
- rotated: float32 [4096, 4096], P(('rows', 'cols'))
Inputs may be any that keep to these rules, and one draw needn't show every extreme that they name: upper is upper triangular: every entry below the diagonal is zero, and every diagonal entry is positive. matching[0] names every block number once; for every row r of matching (round r + 1, r = 0 .. 1), the first block of pair p is that of round 1, matching[r, 2p] = matching[0, 2p], and the second is round 1's second block of pair (p - r) mod (8), matching[r, 2p+1] = matching[0, 2((p - r) mod (8)) + 1].
All inputs are finite; a program needn't handle non-finite values.
Results may differ from a plain program's by a relative error of at most 0.0003.
Values sent between devices are 32-bit elements; how exact they have to be, the bound alone decides.
A program may use at most 128 MiB of HBM per device.

v0:
```python
import jax
import jax.numpy as jnp
from jax import lax
from jax.sharding import PartitionSpec as P

BLK = 256


panel_span = 128


def gram_of(cols_here):
    return lax.dot_general(
        cols_here,
        cols_here,
        (((0,), (0,)), ((), ())),
        precision=lax.Precision.HIGHEST,
        preferred_element_type=jnp.float32,
    )


def product_of(left_mat, right_mat):
    return jnp.dot(
        left_mat, right_mat, precision=lax.Precision.HIGHEST, preferred_element_type=jnp.float32
    )


def blocked_cholesky(gram_mat):
    order_here = gram_mat.shape[0]
    width = min(panel_span, order_here)
    count = order_here // width
    trailing = gram_mat
    columns_out = []
    for panel_index in range(count):
        start = panel_index * width
        diag_part = jnp.linalg.cholesky(trailing[:width, :width])
        below_part = trailing[width:, :width]
        below_factor = jax.scipy.linalg.solve_triangular(diag_part, below_part.T, lower=True).T
        trailing = trailing[width:, width:] - lax.dot_general(
            below_factor,
            below_factor,
            (((1,), (1,)), ((), ())),
            precision=lax.Precision.HIGHEST,
            preferred_element_type=jnp.float32,
        )
        column_panel = jnp.concatenate(
            [jnp.zeros((start, width), jnp.float32), diag_part, below_factor], axis=0
        )
        columns_out.append(column_panel)
    return jnp.concatenate(columns_out, axis=1)


def apply_inverse(work_cols, lower_factor):
    order_here = lower_factor.shape[0]
    width = min(panel_span, order_here)
    count = order_here // width
    solved = []
    for panel_index in range(count):
        start = panel_index * width
        right_side = work_cols[:, start : start + width]
        if panel_index > 0:
            done_cols = jnp.concatenate(solved, axis=1)
            coupling = lower_factor[start : start + width, :start]
            right_side = right_side - lax.dot_general(
                done_cols,
                coupling,
                (((1,), (1,)), ((), ())),
                precision=lax.Precision.HIGHEST,
                preferred_element_type=jnp.float32,
            )
        diag_part = lower_factor[start : start + width, start : start + width]
        solved.append(jax.scipy.linalg.solve_triangular(diag_part, right_side.T, lower=True).T)
    return jnp.concatenate(solved, axis=1)


def orthonormalize(work_cols):
    lower_factor = blocked_cholesky(gram_of(work_cols))
    return apply_inverse(work_cols, lower_factor)


def rotation_of(gram_pair):
    rotation_basis = orthonormalize(gram_pair)
    rotation_basis = orthonormalize(product_of(gram_pair, rotation_basis))
    return rotation_basis


def reorder_blocks(matrix, block_index):
    lead_rows = matrix.shape[0]
    split_view = matrix.reshape(lead_rows, -1, block_index.shape[0], BLK)
    return jnp.take(split_view, block_index, axis=2).reshape(lead_rows, -1)


def local_terms(owned_pair):
    return gram_of(owned_pair)


def summed_gram(gram_terms):
    return lax.psum(gram_terms, "rows")


def pair_round(owned_pair):
    gram_terms = local_terms(owned_pair)
    rotation_basis = rotation_of(summed_gram(gram_terms))
    return product_of(owned_pair, rotation_basis)


def body(upper, matching):
    order_one = matching[0]
    order_two = matching[1]
    inverse_one = jnp.argsort(order_one)
    inverse_two = jnp.argsort(order_two)
    ordered = reorder_blocks(upper, order_one)
    owned_pair = lax.all_to_all(ordered, "cols", split_axis=1, concat_axis=0, tiled=True)
    owned_pair = pair_round(owned_pair)
    regroup_index = inverse_one[order_two]
    spread = lax.all_to_all(owned_pair, "cols", split_axis=0, concat_axis=1, tiled=True)
    spread = reorder_blocks(spread, regroup_index)
    owned_pair = lax.all_to_all(spread, "cols", split_axis=1, concat_axis=0, tiled=True)
    owned_pair = pair_round(owned_pair)
    returned = lax.all_to_all(owned_pair, "cols", split_axis=0, concat_axis=1, tiled=True)
    return reorder_blocks(returned, inverse_two)


def solution(mesh):
    in_specs = (P(("rows", "cols"), None), P())
    out_specs = P(("rows", "cols"), None)
    return jax.shard_map(body, mesh=mesh, in_specs=in_specs, out_specs=out_specs, check_vma=False)
```

profile of v0, /device:TPU:0, one launch (start us, length us, event | category | flops | bytes accessed | tf_op | source)
XLA Modules:
  0.0 779.3 jit_solution(16281866054003176003)
XLA Ops:
  18.6 55.5 %all_to_all.58 = f32[128,8,512]{2,0,1:T(8,128)S(1)} all-to-all(f32[128,8,512]{2,0,1:T(8,128)} %copy.126), channel_id=1, replica_groups=mesh['rows'=4,'cols'=8] {'cols'}, dimensions={1} | all-to-all | bytes 4194304 | tf_op jit(solution)/shard_map/all_to_all | solution.py:113
  75.5 4.7 fusion.8
  80.2 35.2 %all-reduce.3.cloned.1.call-done = f32[512,512]{1,0:T(8,128)} async-done(((f32[512,512]{1,0:T(8,128)}), f32[512,512]{1,0:T(8,128)}) %all-reduce.3.cloned.1.call-update) | async-done | bytes 1048592 | tf_op jit(solution)/shard_map/psum | solution.py:98
  115.4 3.4 fusion.257
  119.0 11.7 %cholesky.254 = f32[128,128]{1,0:T(8,128)S(1)} custom-call(f32[128,128]{1,0:T(8,128)S(1)} %fusion.221), custom_call_target="Cholesky" | custom-call | tf_op jit(solution)/shard_map/jit(cholesky)/cholesky | solution.py:36
  132.2 9.8 %custom-call.38 = f32[1,128,128]{1,2,0:T(8,128)S(1)} custom-call(f32[1,128,128]{2,1,0:T(8,128)S(1)} %get-tuple-element.37), custom_call_target="InvertDiagBlocksLowerTriangular" | custom-call | tf_op jit(solution)/shard_map/jit(_solve_triangular)/triangular_solve | solution.py:72
  143.8 11.7 %cholesky.265 = f32[128,128]{1,0:T(8,128)S(1)} custom-call(f32[128,128]{1,0:T(8,128)S(1)} %fusion.218), custom_call_target="Cholesky" | custom-call | tf_op jit(solution)/shard_map/jit(cholesky)/cholesky | solution.py:36
  157.0 9.8 %custom-call.40 = f32[1,128,128]{1,2,0:T(8,128)S(1)} custom-call(f32[1,128,128]{2,1,0:T(8,128)S(1)} %get-tuple-element.35), custom_call_target="InvertDiagBlocksLowerTriangular" | custom-call | tf_op jit(solution)/shard_map/jit(_solve_triangular)/triangular_solve | solution.py:72
  167.7 11.7 %cholesky.276 = f32[128,128]{1,0:T(8,128)S(1)} custom-call(f32[128,128]{1,0:T(8,128)S(1)} %fusion.215), custom_call_target="Cholesky" | custom-call | tf_op jit(solution)/shard_map/jit(cholesky)/cholesky | solution.py:36
  180.9 10.0 %custom-call.42 = f32[1,128,128]{1,2,0:T(8,128)S(1)} custom-call(f32[1,128,128]{2,1,0:T(8,128)S(1)} %get-tuple-element.33), custom_call_target="InvertDiagBlocksLowerTriangular" | custom-call | tf_op jit(solution)/shard_map/jit(_solve_triangular)/triangular_solve | solution.py:72
  191.8 11.7 %cholesky.287 = f32[128,128]{1,0:T(8,128)S(1)} custom-call(f32[128,128]{1,0:T(8,128)S(1)} %fusion.212), custom_call_target="Cholesky" | custom-call | tf_op jit(solution)/shard_map/jit(cholesky)/cholesky | solution.py:36
  205.0 9.8 %custom-call.44 = f32[1,128,128]{1,2,0:T(8,128)S(1)} custom-call(f32[1,128,128]{2,1,0:T(8,128)S(1)} %fusion.166), custom_call_target="InvertDiagBlocksLowerTriangular" | custom-call | tf_op jit(solution)/shard_map/jit(_solve_triangular)/triangular_solve | solution.py:72
  224.7 11.7 %cholesky.298 = f32[128,128]{1,0:T(8,128)S(1)} custom-call(f32[128,128]{1,0:T(8,128)S(1)} %fusion.210), custom_call_target="Cholesky" | custom-call | tf_op jit(solution)/shard_map/jit(cholesky)/cholesky | solution.py:36
  237.7 9.8 %custom-call.45 = f32[1,128,128]{1,2,0:T(8,128)S(1)} custom-call(f32[1,128,128]{2,1,0:T(8,128)S(1)} %get-tuple-element.31), custom_call_target="InvertDiagBlocksLowerTriangular" | custom-call | tf_op jit(solution)/shard_map/jit(_solve_triangular)/triangular_solve | solution.py:72
  250.1 12.1 %cholesky.309 = f32[128,128]{1,0:T(8,128)S(1)} custom-call(f32[128,128]{1,0:T(8,128)S(1)} %fusion.207), custom_call_target="Cholesky" | custom-call | tf_op jit(solution)/shard_map/jit(cholesky)/cholesky | solution.py:36
  263.6 9.8 %custom-call.47 = f32[1,128,128]{1,2,0:T(8,128)S(1)} custom-call(f32[1,128,128]{2,1,0:T(8,128)S(1)} %get-tuple-element.29), custom_call_target="InvertDiagBlocksLowerTriangular" | custom-call | tf_op jit(solution)/shard_map/jit(_solve_triangular)/triangular_solve | solution.py:72
  274.3 11.7 %cholesky.320 = f32[128,128]{1,0:T(8,128)S(1)} custom-call(f32[128,128]{1,0:T(8,128)S(1)} %fusion.204), custom_call_target="Cholesky" | custom-call | tf_op jit(solution)/shard_map/jit(cholesky)/cholesky | solution.py:36
  287.5 10.0 %custom-call.49 = f32[1,128,128]{1,2,0:T(8,128)S(1)} custom-call(f32[1,128,128]{2,1,0:T(8,128)S(1)} %get-tuple-element.27), custom_call_target="InvertDiagBlocksLowerTriangular" | custom-call | tf_op jit(solution)/shard_map/jit(_solve_triangular)/triangular_solve | solution.py:72
  298.9 11.7 %cholesky.331 = f32[128,128]{1,0:T(8,128)S(1)} custom-call(f32[128,128]{1,0:T(8,128)S(1)} %fusion.201), custom_call_target="Cholesky" | custom-call | tf_op jit(solution)/shard_map/jit(cholesky)/cholesky | solution.py:36
  312.1 9.8 %custom-call.51 = f32[1,128,128]{1,2,0:T(8,128)S(1)} custom-call(f32[1,128,128]{2,1,0:T(8,128)S(1)} %fusion.167), custom_call_target="InvertDiagBlocksLowerTriangular" | custom-call | tf_op jit(solution)/shard_map/jit(_solve_triangular)/triangular_solve | solution.py:72
  326.4 5.2 fusion.4
  331.6 5.6 all-to-all-start.1
  339.3 45.7 %all-to-all-done.1 = f32[8,128,512]{2,1,0:T(8,128)S(1)} async-done(((f32[8,128,512]{2,1,0:T(8,128)}), f32[8,128,512]{2,1,0:T(8,128)S(1)}, u32[]{:S(2)}, u32[]{:S(2)}) %all-to-all-start.1) | async-done | bytes 2097184 | tf_op jit(solution)/shard_map/all_to_all | solution.py:116
  386.8 2.9 copy.156
  397.4 52.0 %all_to_all.59 = f32[128,8,512]{2,0,1:T(8,128)S(1)} all-to-all(f32[128,8,512]{2,0,1:T(8,128)} %copy.158), channel_id=1, replica_groups=mesh['rows'=4,'cols'=8] {'cols'}, dimensions={1} | all-to-all | bytes 4194304 | tf_op jit(solution)/shard_map/all_to_all | solution.py:118
  450.7 4.7 fusion.11
  455.5 35.0 %all-reduce.5.cloned.1.call-done = f32[512,512]{1,0:T(8,128)} async-done(((f32[512,512]{1,0:T(8,128)}), f32[512,512]{1,0:T(8,128)}) %all-reduce.5.cloned.1.call-update) | async-done | bytes 1048592 | tf_op jit(solution)/shard_map/psum | solution.py:98
  490.5 3.4 fusion.259
  494.1 11.7 %cholesky.342 = f32[128,128]{1,0:T(8,128)S(1)} custom-call(f32[128,128]{1,0:T(8,128)S(1)} %fusion.199), custom_call_target="Cholesky" | custom-call | tf_op jit(solution)/shard_map/jit(cholesky)/cholesky | solution.py:36
  507.3 9.8 %custom-call.52 = f32[1,128,128]{1,2,0:T(8,128)S(1)} custom-call(f32[1,128,128]{2,1,0:T(8,128)S(1)} %get-tuple-element.25), custom_call_target="InvertDiagBlocksLowerTriangular" | custom-call | tf_op jit(solution)/shard_map/jit(_solve_triangular)/triangular_solve | solution.py:72
  518.7 11.7 %cholesky.353 = f32[128,128]{1,0:T(8,128)S(1)} custom-call(f32[128,128]{1,0:T(8,128)S(1)} %fusion.196), custom_call_target="Cholesky" | custom-call | tf_op jit(solution)/shard_map/jit(cholesky)/cholesky | solution.py:36
  531.9 9.8 %custom-call.54 = f32[1,128,128]{1,2,0:T(8,128)S(1)} custom-call(f32[1,128,128]{2,1,0:T(8,128)S(1)} %get-tuple-element.23), custom_call_target="InvertDiagBlocksLowerTriangular" | custom-call | tf_op jit(solution)/shard_map/jit(_solve_triangular)/triangular_solve | solution.py:72
  542.6 11.7 %cholesky.364 = f32[128,128]{1,0:T(8,128)S(1)} custom-call(f32[128,128]{1,0:T(8,128)S(1)} %fusion.193), custom_call_target="Cholesky" | custom-call | tf_op jit(solution)/shard_map/jit(cholesky)/cholesky | solution.py:36
  555.8 10.0 %custom-call.56 = f32[1,128,128]{1,2,0:T(8,128)S(1)} custom-call(f32[1,128,128]{2,1,0:T(8,128)S(1)} %get-tuple-element.21), custom_call_target="InvertDiagBlocksLowerTriangular" | custom-call | tf_op jit(solution)/shard_map/jit(_solve_triangular)/triangular_solve | solution.py:72
  566.8 11.7 %cholesky.375 = f32[128,128]{1,0:T(8,128)S(1)} custom-call(f32[128,128]{1,0:T(8,128)S(1)} %fusion.190), custom_call_target="Cholesky" | custom-call | tf_op jit(solution)/shard_map/jit(cholesky)/cholesky | solution.py:36
  579.9 9.8 %custom-call.58 = f32[1,128,128]{1,2,0:T(8,128)S(1)} custom-call(f32[1,128,128]{2,1,0:T(8,128)S(1)} %fusion.168), custom_call_target="InvertDiagBlocksLowerTriangular" | custom-call | tf_op jit(solution)/shard_map/jit(_solve_triangular)/triangular_solve | solution.py:72
  599.8 11.7 %cholesky.386 = f32[128,128]{1,0:T(8,128)S(1)} custom-call(f32[128,128]{1,0:T(8,128)S(1)} %fusion.188), custom_call_target="Cholesky" | custom-call | tf_op jit(solution)/shard_map/jit(cholesky)/cholesky | solution.py:36
  612.8 9.8 %custom-call.59 = f32[1,128,128]{1,2,0:T(8,128)S(1)} custom-call(f32[1,128,128]{2,1,0:T(8,128)S(1)} %get-tuple-element.19), custom_call_target="InvertDiagBlocksLowerTriangular" | custom-call | tf_op jit(solution)/shard_map/jit(_solve_triangular)/triangular_solve | solution.py:72
  625.1 11.9 %cholesky.397 = f32[128,128]{1,0:T(8,128)S(1)} custom-call(f32[128,128]{1,0:T(8,128)S(1)} %fusion.185), custom_call_target="Cholesky" | custom-call | tf_op jit(solution)/shard_map/jit(cholesky)/cholesky | solution.py:36
  638.5 9.8 %custom-call.61 = f32[1,128,128]{1,2,0:T(8,128)S(1)} custom-call(f32[1,128,128]{2,1,0:T(8,128)S(1)} %get-tuple-element.17), custom_call_target="InvertDiagBlocksLowerTriangular" | custom-call | tf_op jit(solution)/shard_map/jit(_solve_triangular)/triangular_solve | solution.py:72
  649.2 11.7 %cholesky.408 = f32[128,128]{1,0:T(8,128)S(1)} custom-call(f32[128,128]{1,0:T(8,128)S(1)} %fusion.182), custom_call_target="Cholesky" | custom-call | tf_op jit(solution)/shard_map/jit(cholesky)/cholesky | solution.py:36
  662.3 10.0 %custom-call.63 = f32[1,128,128]{1,2,0:T(8,128)S(1)} custom-call(f32[1,128,128]{2,1,0:T(8,128)S(1)} %get-tuple-element.14), custom_call_target="InvertDiagBlocksLowerTriangular" | custom-call | tf_op jit(solution)/shard_map/jit(_solve_triangular)/triangular_solve | solution.py:72
  673.8 11.7 %cholesky.419 = f32[128,128]{1,0:T(8,128)S(1)} custom-call(f32[128,128]{1,0:T(8,128)S(1)} %fusion.179), custom_call_target="Cholesky" | custom-call | tf_op jit(solution)/shard_map/jit(cholesky)/cholesky | solution.py:36
  687.0 9.8 %custom-call.65 = f32[1,128,128]{1,2,0:T(8,128)S(1)} custom-call(f32[1,128,128]{2,1,0:T(8,128)S(1)} %fusion.169), custom_call_target="InvertDiagBlocksLowerTriangular" | custom-call | tf_op jit(solution)/shard_map/jit(_solve_triangular)/triangular_solve | solution.py:72
  701.3 5.1 fusion
  706.3 5.5 all-to-all-start.3
  713.2 46.4 %all-to-all-done.3 = f32[8,128,512]{2,1,0:T(8,128)S(1)} async-done(((f32[8,128,512]{2,1,0:T(8,128)}), f32[8,128,512]{2,1,0:T(8,128)S(1)}, u32[]{:S(2)}, u32[]{:S(2)}) %all-to-all-start.3) | async-done | bytes 2097184 | tf_op jit(solution)/shard_map/all_to_all | solution.py:120
  761.4 2.9 copy.188
  (224 shorter events, 105.2 us)
Async XLA Ops:
  6.5 108.9 %all-reduce.3.cloned.1.call-start = ((), (), s32[]{:S(2)}) async-start(), calls=%async_computation.4 | async-start | bytes 2097152 | tf_op jit(solution)/shard_map/psum | solution.py:98
  74.2 1.3 copy-start.2
  143.7 71.2 %copy-start = (f32[512,512]{1,0:T(8,128)S(1)}, f32[512,512]{1,0:T(8,128)}, u32[]{:S(2)}) copy-start(f32[512,512]{1,0:T(8,128)} %all-reduce.3.cloned.1.call-done) | copy-start | bytes 3145732
  323.0 3.4 copy-start.3
  331.6 5.7 copy-start.6
  331.6 53.4 %all-to-all-start.1 = ((f32[8,128,512]{2,1,0:T(8,128)}), f32[8,128,512]{2,1,0:T(8,128)S(1)}, u32[]{:S(2)}, u32[]{:S(2)}) async-start(f32[8,128,512]{2,1,0:T(8,128)} %fusion.4), calls=%async_computation.1 | async-start | bytes 4194304 | tf_op jit(solution)/shard_map/all_to_all | solution.py:116
  337.2 153.3 %all-reduce.5.cloned.1.call-start = ((), (), s32[]{:S(2)}) async-start(), calls=%async_computation.5 | async-start | bytes 2097152 | tf_op jit(solution)/shard_map/psum | solution.py:98
  449.4 1.3 copy-start.4
  518.6 71.3 %copy-start.1 = (f32[512,512]{1,0:T(8,128)S(1)}, f32[512,512]{1,0:T(8,128)}, u32[]{:S(2)}) copy-start(f32[512,512]{1,0:T(8,128)} %all-reduce.5.cloned.1.call-done) | copy-start | bytes 3145732
  697.9 3.4 copy-start.5
  706.3 53.3 %all-to-all-start.3 = ((f32[8,128,512]{2,1,0:T(8,128)}), f32[8,128,512]{2,1,0:T(8,128)S(1)}, u32[]{:S(2)}, u32[]{:S(2)}) async-start(f32[8,128,512]{2,1,0:T(8,128)} %fusion), calls=%async_computation.3 | async-start | bytes 4194304 | tf_op jit(solution)/shard_map/all_to_all | solution.py:120
Sparse Core Ops, SparseCore 0:
  80.3 35.0 all-reduce.2
  455.6 34.8 all-reduce.4
where the time goes:
time: 790 us; the launch traced here: 779 us
  other arithmetic  377 us (48%)
  waiting for transfers between devices  162 us (21%)
  blocking collectives  108 us (14%)
  matrix products  63.6 us (8%)
  local copies, waits for them, and re-layouts  42.4 us (5%)
  between operations  15.2 us (2%)
  starting transfers between devices  11.2 us (1%)
    another operation x48, other arithmetic, blocked_cholesky(): diag_part = jnp.linalg.cholesky(trailing[:width, :width])  200 us
    another operation x32, other arithmetic, apply_inverse(): jax.scipy.linalg.solve_triangular(diag_part, right_side.T, lower=True)  169 us
    all_to_all x2, waiting for transfers between devices, body(): lax.all_to_all(owned_pair, 'cols', split_axis=0, concat_axis=1, tiled=True)  92.1 us
    psum x2, waiting for transfers between devices, summed_gram(): return lax.psum(gram_terms, 'rows')  70.3 us
    all_to_all x1, blocking collectives, body(): lax.all_to_all(ordered, 'cols', split_axis=1, concat_axis=0, tiled=True)  55.5 us
    all_to_all x1, blocking collectives, body(): lax.all_to_all(spread, 'cols', split_axis=1, concat_axis=0, tiled=True)  52 us
    dot_general x6, matrix products, gram_of(): lax.dot_general(cols_here, cols_here, (((0,), (0,)), ((), ())), precision...  19.9 us
  transfers between devices with their start and end apart: 4, of which 4 were waited for; matrix products, arithmetic and copies ran while one was open for 0% of the time, Pallas kernels for 0%

commit v1 on v0

--- a/solution.py
+++ b/solution.py
@@ -1,6 +1,9 @@
 import jax
 import jax.numpy as jnp
+import numpy as np
 from jax import lax
+from jax.experimental import pallas as pl
+from jax.experimental.pallas import tpu as pltpu
 from jax.sharding import PartitionSpec as P
 
 BLK = 256
@@ -84,44 +87,82 @@
     return rotation_basis
 
 
-def reorder_blocks(matrix, block_index):
-    lead_rows = matrix.shape[0]
-    split_view = matrix.reshape(lead_rows, -1, block_index.shape[0], BLK)
-    return jnp.take(split_view, block_index, axis=2).reshape(lead_rows, -1)
+def copy_kernel(order_ref, src_ref, dst_ref):
+    dst_ref[...] = src_ref[...].reshape(dst_ref.shape)
 
 
-def local_terms(owned_pair):
-    return gram_of(owned_pair)
+def pack_blocks(matrix, order):
+    rows, width = matrix.shape
+    count = width // BLK
+    return pl.pallas_call(
+        copy_kernel,
+        out_shape=jax.ShapeDtypeStruct((count // 2, rows, 2 * BLK), jnp.float32),
+        grid_spec=pltpu.PrefetchScalarGridSpec(
+            num_scalar_prefetch=1,
+            grid=(count,),
+            in_specs=[pl.BlockSpec((rows, BLK), lambda i, order: (0, order[i]))],
+            out_specs=pl.BlockSpec((1, rows, BLK), lambda i, order: (i // 2, 0, i % 2)),
+        ),
+    )(order, matrix)
 
 
-def summed_gram(gram_terms):
-    return lax.psum(gram_terms, "rows")
+def unpack_blocks(packed, order):
+    pairs, rows, _ = packed.shape
+    count = 2 * pairs
+    return pl.pallas_call(
+        copy_kernel,
+        out_shape=jax.ShapeDtypeStruct((rows, count * BLK), jnp.float32),
+        grid_spec=pltpu.PrefetchScalarGridSpec(
+            num_scalar_prefetch=1,
+            grid=(count,),
+            in_specs=[pl.BlockSpec((1, rows, BLK), lambda i, order: (i // 2, 0, i % 2))],
+            out_specs=pl.BlockSpec((rows, BLK), lambda i, order: (0, order[i])),
+        ),
+    )(order, packed)
+
+
+def pair_places(count):
+    half = count // 2
+    return [2 * k if k < half else 2 * (count - 1 - k) + 1 for k in range(count)]
 
 
 def pair_round(owned_pair):
-    gram_terms = local_terms(owned_pair)
-    rotation_basis = rotation_of(summed_gram(gram_terms))
+    gram_terms = gram_of(owned_pair)
+    rotation_basis = rotation_of(lax.psum(gram_terms, "rows"))
     return product_of(owned_pair, rotation_basis)
 
 
-def body(upper, matching):
-    order_one = matching[0]
-    order_two = matching[1]
-    inverse_one = jnp.argsort(order_one)
-    inverse_two = jnp.argsort(order_two)
-    ordered = reorder_blocks(upper, order_one)
-    owned_pair = lax.all_to_all(ordered, "cols", split_axis=1, concat_axis=0, tiled=True)
-    owned_pair = pair_round(owned_pair)
-    regroup_index = inverse_one[order_two]
-    spread = lax.all_to_all(owned_pair, "cols", split_axis=0, concat_axis=1, tiled=True)
-    spread = reorder_blocks(spread, regroup_index)
-    owned_pair = lax.all_to_all(spread, "cols", split_axis=1, concat_axis=0, tiled=True)
-    owned_pair = pair_round(owned_pair)
-    returned = lax.all_to_all(owned_pair, "cols", split_axis=0, concat_axis=1, tiled=True)
-    return reorder_blocks(returned, inverse_two)
+def exchange(chunks):
+    return lax.all_to_all(chunks, "cols", split_axis=0, concat_axis=0, tiled=True)
+
+
+def make_body(count):
+    places = pair_places(count)
+    pair_at = np.argsort(np.array(places))
+    slots = np.stack([2 * pair_at, 2 * pair_at + 1], axis=1).reshape(-1)
+    ring = [(places[k], places[(k + 1) % count]) for k in range(count)]
+
+    def body(upper, matching):
+        rows = upper.shape[0]
+        chunks = exchange(pack_blocks(upper, matching[0][slots]))
+        owned = chunks.reshape(count * rows, 2 * BLK)
+        owned = pair_round(owned)
+        second = lax.ppermute(owned[:, BLK:], "cols", ring)
+        owned = jnp.concatenate([owned[:, :BLK], second], axis=1)
+        owned = pair_round(owned)
+        returned = exchange(owned.reshape(count, rows, 2 * BLK))
+        return unpack_blocks(returned, matching[1][slots])
+
+    return body
 
 
 def solution(mesh):
     in_specs = (P(("rows", "cols"), None), P())
     out_specs = P(("rows", "cols"), None)
-    return jax.shard_map(body, mesh=mesh, in_specs=in_specs, out_specs=out_specs, check_vma=False)
+    return jax.shard_map(
+        make_body(mesh.shape["cols"]),
+        mesh=mesh,
+        in_specs=in_specs,
+        out_specs=out_specs,
+        check_vma=False,
+    )

time: 790 us -> 778 us (0.985)
  blocking collectives: 108 us -> 55.5 us
  other arithmetic: 377 us -> 402 us
  matrix products: 63.6 us -> 87.4 us
  Pallas kernels: 0 us -> 20.3 us
  waiting for transfers between devices: 162 us -> 142 us
    all_to_all x2 -> x1, blocking collectives: 108 us -> 55.5 us  [exchange(): lax.all_to_all(chunks, 'cols', split_axis=0, concat_axis=0, tiled=True)]
    all_to_all x2 -> x1, waiting for transfers between devices: 92.1 us -> 46.6 us  [exchange(): lax.all_to_all(chunks, 'cols', split_axis=0, concat_axis=0, tiled=True)]
    ppermute x0 -> x1, waiting for transfers between devices: none -> 23.2 us  [body(): second = lax.ppermute(owned[:, BLK:], 'cols', ring)]
    pallas_call x0 -> x2, Pallas kernels: none -> 20.3 us  [the longest x1 10.2 us: pack_blocks(): pl.pallas_call(copy_kernel, out_shape=jax.ShapeDtypeStruct((count // 2, r...]
    another operation x32, other arithmetic: 169 us -> 184 us  [apply_inverse(): jax.scipy.linalg.solve_triangular(diag_part, right_side.T, lower=True)]
    reshape x4 -> x0, local copies, waits for them, and re-layouts: 9.51 us -> none  [the longest x3 7.7 us: reorder_blocks(): split_view = matrix.reshape(lead_rows, -1, block_index.shape[0], BLK)]
    div x16, other arithmetic: 0.22 us -> 9.65 us  [blocked_cholesky(): diag_part = jnp.linalg.cholesky(trailing[:width, :width])]
    select_n x12, local copies, waits for them, and re-layouts: 1.09 us -> 9.28 us  [blocked_cholesky(): diag_part = jnp.linalg.cholesky(trailing[:width, :width])]
where the time goes in v1:
time: 778 us; the launch traced here: 771 us
  other arithmetic  402 us (52%)
  waiting for transfers between devices  142 us (18%)
  matrix products  87.4 us (11%)
  blocking collectives  55.5 us (7%)
  local copies, waits for them, and re-layouts  41.9 us (5%)
  Pallas kernels  20.3 us (3%)
  between operations  15 us (2%)
    another operation x48, other arithmetic, blocked_cholesky(): diag_part = jnp.linalg.cholesky(trailing[:width, :width])  208 us
    another operation x32, other arithmetic, apply_inverse(): jax.scipy.linalg.solve_triangular(diag_part, right_side.T, lower=True)  184 us
    psum x2, waiting for transfers between devices, pair_round(): rotation_basis = rotation_of(lax.psum(gram_terms, 'rows'))  71.7 us
    all_to_all x1, blocking collectives, exchange(): lax.all_to_all(chunks, 'cols', split_axis=0, concat_axis=0, tiled=True)  55.5 us
    all_to_all x1, waiting for transfers between devices, exchange(): lax.all_to_all(chunks, 'cols', split_axis=0, concat_axis=0, tiled=True)  46.6 us
    ppermute x1, waiting for transfers between devices, body(): second = lax.ppermute(owned[:, BLK:], 'cols', ring)  23.2 us
    dot_general x6, matrix products, gram_of(): lax.dot_general(cols_here, cols_here, (((0,), (0,)), ((), ())), precision...  19.9 us
    dot_general x12, matrix products, apply_inverse(): lax.dot_general(done_cols, coupling, (((1,), (1,)), ((), ())), precision=...  16 us
  transfers between devices with their start and end apart: 4, of which 4 were waited for; matrix products, arithmetic and copies ran while one was open for 0% of the time, Pallas kernels for 0%

profile of v1, /device:TPU:0, one launch (start us, length us, event | category | flops | bytes accessed | tf_op | source)
XLA Modules:
  0.0 771.3 jit_solution(14921062506281250860)
XLA Ops:
  9.2 10.2 %shard_map.55 = f32[8,128,512]{2,1,0:T(8,128)} custom-call(s32[16]{0:T(128)} %gather_fusion.1, f32[128,4096]{1,0:T(8,128)} %src_ref.1), custom_call_target="tpu_custom_call" | custom-call | tf_op jit(solution)/shard_map/pallas_call | solution.py:97
  19.4 55.5 %all_to_all.10 = f32[8,128,512]{2,1,0:T(8,128)S(1)} all-to-all(f32[8,128,512]{2,1,0:T(8,128)} %shard_map.55), channel_id=1, replica_groups=mesh['rows'=4,'cols'=8] {'cols'}, dimensions={0} | all-to-all | bytes 4194304 | tf_op jit(solution)/shard_map/all_to_all | solution.py:136
  74.9 4.6 convolution_bitcast_fusion
  79.8 35.0 %all-reduce.3.cloned.1.call-done = f32[512,512]{1,0:T(8,128)} async-done(((f32[512,512]{1,0:T(8,128)}), f32[512,512]{1,0:T(8,128)}) %all-reduce.3.cloned.1.call-update) | async-done | bytes 1048592 | tf_op jit(solution)/shard_map/psum | solution.py:131
  114.8 3.4 fusion.255
  119.2 11.7 %cholesky.254 = f32[128,128]{1,0:T(8,128)S(1)} custom-call(f32[128,128]{1,0:T(8,128)S(1)} %fusion.218), custom_call_target="Cholesky" | custom-call | tf_op jit(solution)/shard_map/jit(cholesky)/cholesky | solution.py:39
  133.0 9.8 %custom-call.38 = f32[1,128,128]{1,2,0:T(8,128)S(1)} custom-call(f32[1,128,128]{2,1,0:T(8,128)S(1)} %get-tuple-element.32), custom_call_target="InvertDiagBlocksLowerTriangular" | custom-call | tf_op jit(solution)/shard_map/jit(_solve_triangular)/triangular_solve | solution.py:75
  147.1 11.9 %cholesky.265 = f32[128,128]{1,0:T(8,128)S(1)} custom-call(f32[128,128]{1,0:T(8,128)S(1)} %fusion.215), custom_call_target="Cholesky" | custom-call | tf_op jit(solution)/shard_map/jit(cholesky)/cholesky | solution.py:39
  161.0 10.6 %custom-call.40 = f32[1,128,128]{1,2,0:T(8,128)S(1)} custom-call(f32[1,128,128]{2,1,0:T(8,128)} %get-tuple-element.30), custom_call_target="InvertDiagBlocksLowerTriangular" | custom-call | tf_op jit(solution)/shard_map/jit(_solve_triangular)/triangular_solve | solution.py:75
  178.7 13.2 %cholesky.276 = f32[128,128]{1,0:T(8,128)} custom-call(f32[128,128]{1,0:T(8,128)} %fusion.212), custom_call_target="Cholesky" | custom-call | tf_op jit(solution)/shard_map/jit(cholesky)/cholesky | solution.py:39
  195.5 11.3 %custom-call.42 = f32[1,128,128]{1,2,0:T(8,128)} custom-call(f32[1,128,128]{2,1,0:T(8,128)} %get-tuple-element.28), custom_call_target="InvertDiagBlocksLowerTriangular" | custom-call | tf_op jit(solution)/shard_map/jit(_solve_triangular)/triangular_solve | solution.py:75
  216.0 13.5 %cholesky.287 = f32[128,128]{1,0:T(8,128)} custom-call(f32[128,128]{1,0:T(8,128)} %fusion.209), custom_call_target="Cholesky" | custom-call | tf_op jit(solution)/shard_map/jit(cholesky)/cholesky | solution.py:39
  233.2 11.3 %custom-call.44 = f32[1,128,128]{1,2,0:T(8,128)} custom-call(f32[1,128,128]{2,1,0:T(8,128)} %fusion.162), custom_call_target="InvertDiagBlocksLowerTriangular" | custom-call | tf_op jit(solution)/shard_map/jit(_solve_triangular)/triangular_solve | solution.py:75
  259.5 11.7 %cholesky.298 = f32[128,128]{1,0:T(8,128)S(1)} custom-call(f32[128,128]{1,0:T(8,128)S(1)} %fusion.207), custom_call_target="Cholesky" | custom-call | tf_op jit(solution)/shard_map/jit(cholesky)/cholesky | solution.py:39
  273.1 9.8 %custom-call.45 = f32[1,128,128]{1,2,0:T(8,128)S(1)} custom-call(f32[1,128,128]{2,1,0:T(8,128)S(1)} %get-tuple-element.26), custom_call_target="InvertDiagBlocksLowerTriangular" | custom-call | tf_op jit(solution)/shard_map/jit(_solve_triangular)/triangular_solve | solution.py:75
  283.4 2.2 copy.128
  291.2 12.5 %cholesky.309 = f32[128,128]{1,0:T(8,128)S(1)} custom-call(f32[128,128]{1,0:T(8,128)} %fusion.204), custom_call_target="Cholesky" | custom-call | tf_op jit(solution)/shard_map/jit(cholesky)/cholesky | solution.py:39
  306.0 10.6 %custom-call.47 = f32[1,128,128]{1,2,0:T(8,128)S(1)} custom-call(f32[1,128,128]{2,1,0:T(8,128)} %get-tuple-element.24), custom_call_target="InvertDiagBlocksLowerTriangular" | custom-call | tf_op jit(solution)/shard_map/jit(_solve_triangular)/triangular_solve | solution.py:75
  323.0 11.7 %cholesky.320 = f32[128,128]{1,0:T(8,128)S(1)} custom-call(f32[128,128]{1,0:T(8,128)S(1)} %fusion.201), custom_call_target="Cholesky" | custom-call | tf_op jit(solution)/shard_map/jit(cholesky)/cholesky | solution.py:39
  336.8 9.8 %custom-call.49 = f32[1,128,128]{1,2,0:T(8,128)S(1)} custom-call(f32[1,128,128]{2,1,0:T(8,128)S(1)} %get-tuple-element.22), custom_call_target="InvertDiagBlocksLowerTriangular" | custom-call | tf_op jit(solution)/shard_map/jit(_solve_triangular)/triangular_solve | solution.py:75
  356.2 13.6 %cholesky.331 = f32[128,128]{1,0:T(8,128)} custom-call(f32[128,128]{1,0:T(8,128)} %fusion.198), custom_call_target="Cholesky" | custom-call | tf_op jit(solution)/shard_map/jit(cholesky)/cholesky | solution.py:39
  373.5 11.3 %custom-call.51 = f32[1,128,128]{1,2,0:T(8,128)} custom-call(f32[1,128,128]{2,1,0:T(8,128)} %fusion.163), custom_call_target="InvertDiagBlocksLowerTriangular" | custom-call | tf_op jit(solution)/shard_map/jit(_solve_triangular)/triangular_solve | solution.py:75
  393.6 3.6 fusion.19
  399.0 23.2 %collective-permute-done = f32[1024,256]{0,1:T(8,128)S(1)} collective-permute-done((f32[1024,256]{0,1:T(8,128)S(1)}, f32[1024,256]{0,1:T(8,128)S(1)}, u32[]{:S(2)}, u32[]{:S(2)}) %collective-permute-start) | collective-permute-done | bytes 1048608 | tf_op jit(solution)/shard_map/ppermute | solution.py:150
  423.1 4.6 fusion.1
  427.8 36.7 %all-reduce.5.cloned.1.call-done = f32[512,512]{1,0:T(8,128)} async-done(((f32[512,512]{1,0:T(8,128)}), f32[512,512]{1,0:T(8,128)}) %all-reduce.5.cloned.1.call-update) | async-done | bytes 1048592 | tf_op jit(solution)/shard_map/psum | solution.py:131
  464.4 3.4 fusion.257
  468.0 11.7 %cholesky.342 = f32[128,128]{1,0:T(8,128)S(1)} custom-call(f32[128,128]{1,0:T(8,128)S(1)} %fusion.196), custom_call_target="Cholesky" | custom-call | tf_op jit(solution)/shard_map/jit(cholesky)/cholesky | solution.py:39
  481.7 9.8 %custom-call.52 = f32[1,128,128]{1,2,0:T(8,128)S(1)} custom-call(f32[1,128,128]{2,1,0:T(8,128)S(1)} %get-tuple-element.20), custom_call_target="InvertDiagBlocksLowerTriangular" | custom-call | tf_op jit(solution)/shard_map/jit(_solve_triangular)/triangular_solve | solution.py:75
  494.9 11.7 %cholesky.353 = f32[128,128]{1,0:T(8,128)S(1)} custom-call(f32[128,128]{1,0:T(8,128)S(1)} %fusion.193), custom_call_target="Cholesky" | custom-call | tf_op jit(solution)/shard_map/jit(cholesky)/cholesky | solution.py:39
  508.0 9.8 %custom-call.54 = f32[1,128,128]{1,2,0:T(8,128)S(1)} custom-call(f32[1,128,128]{2,1,0:T(8,128)S(1)} %get-tuple-element.18), custom_call_target="InvertDiagBlocksLowerTriangular" | custom-call | tf_op jit(solution)/shard_map/jit(_solve_triangular)/triangular_solve | solution.py:75
  520.6 11.7 %cholesky.364 = f32[128,128]{1,0:T(8,128)S(1)} custom-call(f32[128,128]{1,0:T(8,128)S(1)} %fusion.190), custom_call_target="Cholesky" | custom-call | tf_op jit(solution)/shard_map/jit(cholesky)/cholesky | solution.py:39
  533.7 10.2 %custom-call.56 = f32[1,128,128]{1,2,0:T(8,128)S(1)} custom-call(f32[1,128,128]{2,1,0:T(8,128)S(1)} %get-tuple-element.16), custom_call_target="InvertDiagBlocksLowerTriangular" | custom-call | tf_op jit(solution)/shard_map/jit(_solve_triangular)/triangular_solve | solution.py:75
  545.5 11.7 %cholesky.375 = f32[128,128]{1,0:T(8,128)S(1)} custom-call(f32[128,128]{1,0:T(8,128)S(1)} %fusion.187), custom_call_target="Cholesky" | custom-call | tf_op jit(solution)/shard_map/jit(cholesky)/cholesky | solution.py:39
  558.5 10.4 %custom-call.58 = f32[1,128,128]{1,2,0:T(8,128)} custom-call(f32[1,128,128]{2,1,0:T(8,128)S(1)} %fusion.164), custom_call_target="InvertDiagBlocksLowerTriangular" | custom-call | tf_op jit(solution)/shard_map/jit(_solve_triangular)/triangular_solve | solution.py:75
  580.5 11.7 %cholesky.386 = f32[128,128]{1,0:T(8,128)S(1)} custom-call(f32[128,128]{1,0:T(8,128)S(1)} %fusion.185), custom_call_target="Cholesky" | custom-call | tf_op jit(solution)/shard_map/jit(cholesky)/cholesky | solution.py:39
  594.2 9.8 %custom-call.59 = f32[1,128,128]{1,2,0:T(8,128)S(1)} custom-call(f32[1,128,128]{2,1,0:T(8,128)S(1)} %get-tuple-element.14), custom_call_target="InvertDiagBlocksLowerTriangular" | custom-call | tf_op jit(solution)/shard_map/jit(_solve_triangular)/triangular_solve | solution.py:75
  608.2 11.9 %cholesky.397 = f32[128,128]{1,0:T(8,128)S(1)} custom-call(f32[128,128]{1,0:T(8,128)S(1)} %fusion.182), custom_call_target="Cholesky" | custom-call | tf_op jit(solution)/shard_map/jit(cholesky)/cholesky | solution.py:39
  621.4 9.8 %custom-call.61 = f32[1,128,128]{1,2,0:T(8,128)S(1)} custom-call(f32[1,128,128]{2,1,0:T(8,128)S(1)} %get-tuple-element.10), custom_call_target="InvertDiagBlocksLowerTriangular" | custom-call | tf_op jit(solution)/shard_map/jit(_solve_triangular)/triangular_solve | solution.py:75
  634.6 11.7 %cholesky.408 = f32[128,128]{1,0:T(8,128)S(1)} custom-call(f32[128,128]{1,0:T(8,128)S(1)} %fusion.179), custom_call_target="Cholesky" | custom-call | tf_op jit(solution)/shard_map/jit(cholesky)/cholesky | solution.py:39
  647.7 10.2 %custom-call.63 = f32[1,128,128]{1,2,0:T(8,128)S(1)} custom-call(f32[1,128,128]{2,1,0:T(8,128)S(1)} %get-tuple-element.6), custom_call_target="InvertDiagBlocksLowerTriangular" | custom-call | tf_op jit(solution)/shard_map/jit(_solve_triangular)/triangular_solve | solution.py:75
  660.0 11.7 %cholesky.419 = f32[128,128]{1,0:T(8,128)S(1)} custom-call(f32[128,128]{1,0:T(8,128)S(1)} %fusion.176), custom_call_target="Cholesky" | custom-call | tf_op jit(solution)/shard_map/jit(cholesky)/cholesky | solution.py:39
  673.0 10.4 %custom-call.65 = f32[1,128,128]{1,2,0:T(8,128)} custom-call(f32[1,128,128]{2,1,0:T(8,128)S(1)} %fusion.165), custom_call_target="InvertDiagBlocksLowerTriangular" | custom-call | tf_op jit(solution)/shard_map/jit(_solve_triangular)/triangular_solve | solution.py:75
  688.3 2.3 fusion.8
  691.1 8.4 %fusion = f32[1024,512]{1,0:T(8,128)} fusion(f32[1024,256]{0,1:T(8,128)S(1)} %copy-done.20, f32[1024,256]{0,1:T(8,128)S(1)} %get-tuple-element.34, f32[512,128]{0,1:T(8,128)S(1)} %convolution_bitcast_fusion.1, f32[512,128]{0,1:T(8,128)S(1)} %convolution_bitcast_fusion.2, f32[512,128]{0,1:T(8,128)S(1)} %convolution_bitcast_fusion.3, f32[512,128]{0,1:T(8,128)S(1)} %bitcast.371), kind=kOutput, calls=%fused_computation.3 | convolution fusion | flops 3222536192 | bytes 5242880 | tf_op jit(solution)/shard_map/dot_general | solution.py:26
  699.5 5.5 all-to-all-start.1
  706.2 46.6 %all-to-all-done.1.src_ref = f32[8,128,512]{2,1,0:T(8,128)S(1)} async-done(((f32[8,128,512]{2,1,0:T(8,128)}), f32[8,128,512]{2,1,0:T(8,128)S(1)}, u32[]{:S(2)}, u32[]{:S(2)}) %all-to-all-start.1) | async-done | bytes 2097184 | tf_op jit(solution)/shard_map/all_to_all | solution.py:136
  754.2 10.2 %shard_map.56 = f32[128,4096]{1,0:T(8,128)} custom-call(s32[16]{0:T(128)} %gather_fusion, f32[8,128,512]{2,1,0:T(8,128)} %copy-done.4), custom_call_target="tpu_custom_call" | custom-call | tf_op jit(solution)/shard_map/pallas_call | solution.py:112
  (274 shorter events, 142.4 us)
Async XLA Ops:
  6.5 108.3 %all-reduce.3.cloned.1.call-start = ((), (), s32[]{:S(2)}) async-start(), calls=%async_computation.2 | async-start | bytes 2097152 | tf_op jit(solution)/shard_map/psum | solution.py:131
  79.5 384.9 %all-reduce.5.cloned.1.call-start = ((), (), s32[]{:S(2)}) async-start(), calls=%async_computation.3 | async-start | bytes 2097152 | tf_op jit(solution)/shard_map/psum | solution.py:131
  142.8 18.2 %copy-start.25 = (f32[1,128,128]{1,2,0:T(8,128)}, f32[1,128,128]{1,2,0:T(8,128)S(1)}, u32[]{:S(2)}) copy-start(f32[1,128,128]{1,2,0:T(8,128)S(1)} %custom-call.38) | copy-start | bytes 196612
  145.2 0.8 copy-start.15
  146.0 100.0 %copy-start.1 = (f32[512,512]{1,0:T(8,128)S(1)}, f32[512,512]{1,0:T(8,128)}, u32[]{:S(2)}) copy-start(f32[512,512]{1,0:T(8,128)} %all-reduce.3.cloned.1.call-done) | copy-start | bytes 3145732
  171.6 23.9 %copy-start.26 = (f32[1,128,128]{1,2,0:T(8,128)}, f32[1,128,128]{1,2,0:T(8,128)S(1)}, u32[]{:S(2)}) copy-start(f32[1,128,128]{1,2,0:T(8,128)S(1)} %custom-call.40) | copy-start | bytes 196612
  172.9 75.0 %copy-start.11 = (f32[128,256]{1,0:T(8,128)}, f32[128,256]{1,0:T(8,128)S(1)}, u32[]{:S(2)}) copy-start(f32[128,256]{1,0:T(8,128)S(1)} %fusion.161) | copy-start | bytes 393220
  174.3 0.7 copy-start.21
  246.0 3.2 copy-start.23
  246.0 5.2 copy-start.29
  246.0 5.6 copy-start.35
  246.0 5.6 copy-start.37
  249.2 2.4 copy-start.12
  249.2 3.9 copy-start.42
  251.6 1.5 copy-start.7
  255.4 1.0 copy-start.2
  283.4 36.5 %copy-start.5 = (f32[128,384]{1,0:T(8,128)}, f32[128,384]{1,0:T(8,128)S(1)}, u32[]{:S(2)}) copy-start(f32[128,384]{1,0:T(8,128)S(1)} %fusion.127) | copy-start | bytes 589828
  285.6 64.7 %copy-start.3 = (f32[512,512]{1,0:T(8,128)S(1)}, f32[512,512]{1,0:T(8,128)}, u32[]{:S(2)}) copy-start(f32[512,512]{1,0:T(8,128)} %copy-done.2) | copy-start | bytes 3145732
  287.4 0.8 copy-start.16
  316.6 32.9 %copy-start.27 = (f32[1,128,128]{1,2,0:T(8,128)}, f32[1,128,128]{1,2,0:T(8,128)S(1)}, u32[]{:S(2)}) copy-start(f32[1,128,128]{1,2,0:T(8,128)S(1)} %custom-call.47) | copy-start | bytes 196612
  317.9 0.6 copy-start.13
  319.9 0.7 copy-start.22
  346.6 2.9 copy-start.30
  386.4 4.7 copy-start.31
  386.4 5.2 copy-start.6
  386.4 5.2 copy-start.8
  386.4 5.2 copy-start.14
  386.4 5.2 copy-start.24
  386.4 5.2 copy-start.36
  386.4 5.2 copy-start.39
  389.2 4.0 copy-start.44
  397.3 24.9 %collective-permute-start = (f32[1024,256]{0,1:T(8,128)S(1)}, f32[1024,256]{0,1:T(8,128)S(1)}, u32[]{:S(2)}, u32[]{:S(2)}) collective-permute-start(f32[1024,256]{0,1:T(8,128)S(1)} %get-tuple-element.35), channel_id=1, source_target_pairs={{0,2},{2,4},{4,6},{6,7},{7,5},{5,3},{3,1},{1,0},{8,10},{10,12},{12... | collective-permute-start | bytes 3145736 | tf_op jit(solution)/shard_map/ppermute | solution.py:150
  422.2 1.0 copy-start.19
  492.4 52.8 %copy-start.34 = (f32[128,128]{1,0:T(8,128)S(1)}, f32[128,128]{1,0:T(8,128)}, u32[]{:S(2)}) copy-start(f32[128,128]{1,0:T(8,128)} %get-tuple-element.21) | copy-start | bytes 196612
  493.1 0.8 copy-start.17
  493.9 75.1 %copy-start = (f32[512,512]{1,0:T(8,128)S(1)}, f32[512,512]{1,0:T(8,128)}, u32[]{:S(2)}) copy-start(f32[512,512]{1,0:T(8,128)} %all-reduce.5.cloned.1.call-done) | copy-start | bytes 3145732
  517.8 2.6 copy-start.40
  543.9 0.6 copy-start.41
  569.0 4.6 copy-start.9
  571.3 4.0 copy-start.45
  606.4 0.8 copy-start.18
  607.2 52.5 %copy-start.33 = (f32[128,128]{1,0:T(8,128)S(1)}, f32[128,128]{1,0:T(8,128)}, u32[]{:S(2)}) copy-start(f32[128,128]{1,0:T(8,128)} %get-tuple-element.15) | copy-start | bytes 196612
  660.0 28.3 %copy-start.10 = (f32[256,128]{0,1:T(8,128)S(1)}, f32[256,128]{0,1:T(8,128)}, u32[]{:S(2)}) copy-start(f32[256,128]{0,1:T(8,128)} %copy-done.7) | copy-start | bytes 393220
  684.2 4.2 copy-start.38
  686.0 4.7 copy-start.43
  686.0 5.1 copy-start.20
  699.5 53.3 %all-to-all-start.1 = ((f32[8,128,512]{2,1,0:T(8,128)}), f32[8,128,512]{2,1,0:T(8,128)S(1)}, u32[]{:S(2)}, u32[]{:S(2)}) async-start(f32[8,128,512]{2,1,0:T(8,128)} %bitcast.132), calls=%async_computation.1 | async-start | bytes 4194304 | tf_op jit(solution)/shard_map/all_to_all | solution.py:136
  752.8 1.4 copy-start.4
  (2 other events, 1.2 us)
Sparse Core Ops, SparseCore 0:
  79.7 35.0 all-reduce.2
  427.9 36.5 all-reduce.4

commit v2 on v1

v2 whole, which is shorter than its diff:
```python
import functools

import jax
import jax.numpy as jnp
import numpy as np
from jax import lax
from jax.experimental import pallas as pl
from jax.experimental.pallas import tpu as pltpu
from jax.sharding import PartitionSpec as P

BLK = 256
HIGH = lax.Precision.HIGHEST
SUB, WIDE = 8, 128


def wide(part):
    return jnp.broadcast_to(part, (SUB, WIDE))


def factor_panel(diag):
    count = WIDE // SUB
    row = lax.broadcasted_iota(jnp.int32, (SUB, WIDE), 0)
    lane = lax.broadcasted_iota(jnp.int32, (SUB, WIDE), 1)
    left = [diag[SUB * k : SUB * (k + 1), :] for k in range(count)]
    right = [jnp.where(lane == row + SUB * k, 1.0, 0.0) for k in range(count)]

    def columns_of(tile, b):
        return [wide(tile[:, SUB * b + i : SUB * b + i + 1]) for i in range(SUB)]

    for b in range(count):
        here, mirror = left[b], right[b]
        cols = columns_of(here, b)
        scale = jnp.zeros((SUB, WIDE), jnp.float32)
        left_rows, right_rows, pivots, cross = [], [], [], []
        for i in range(SUB):
            root = lax.rsqrt(wide(cols[i][i : i + 1, :]))
            inverse = root * root
            scale = jnp.where(row == i, root, scale)
            left_rows.append(wide(here[i : i + 1, :]))
            right_rows.append(wide(mirror[i : i + 1, :]))
            pivots.append(inverse)
            cross.append([wide(cols[j][i : i + 1, :]) for j in range(i + 1, SUB)])
            if i + 1 < SUB:
                factor = jnp.where(row > i, cols[i] * inverse, 0.0)
                for j in range(i + 1, SUB):
                    cols[j] = cols[j] - factor * cross[i][j - i - 1]
                here = here - factor * left_rows[i]
                mirror = mirror - factor * right_rows[i]
        right[b] = mirror * scale
        for k in range(b + 1, count):
            below = columns_of(left[k], b)
            for i in range(SUB):
                factor = below[i] * pivots[i]
                for j in range(i + 1, SUB):
                    below[j] = below[j] - factor * cross[i][j - i - 1]
                left[k] = left[k] - factor * left_rows[i]
                right[k] = right[k] - factor * right_rows[i]
    return jnp.concatenate(right, axis=0)


def mul(a, b, dims):
    return lax.dot_general(
        a, b, (dims, ((), ())), precision=HIGH, preferred_element_type=jnp.float32
    )


def rotation_kernel(steps, gram_ref, turn_ref, work_ref, inv_ref):
    n = gram_ref.shape[0]
    count = n // WIDE

    def panel(t, carry):
        p = lax.rem(t, count)

        @pl.when(t == 0)
        def _():
            work_ref[:, n:] = gram_ref[...]

        @pl.when(jnp.logical_and(p == 0, t > 0))
        def _():
            work_ref[:, n:] = mul(work_ref[:, n:], gram_ref[...], ((1,), (0,)))

        @pl.when(p == 0)
        def _():
            work_ref[:, :n] = mul(work_ref[:, n:], work_ref[:, n:], ((1,), (1,)))

        at = pl.ds(pl.multiple_of(p * WIDE, WIDE), WIDE)
        inv_ref[...] = factor_panel(work_ref[at, at])
        for q in range(count):

            @pl.when(p == q)
            def _():
                lo, hi = q * WIDE, (q + 1) * WIDE
                rows = mul(inv_ref[...], work_ref[lo:hi, hi:], ((1,), (0,)))
                work_ref[lo:hi, hi:] = rows
                if q + 1 < count:
                    work_ref[hi:, hi:] -= mul(rows[:, : n - hi], rows, ((0,), (0,)))

        return carry

    lax.fori_loop(0, steps * count, panel, 0)
    turn_ref[...] = work_ref[:, n:]


def rotation_of(gram):
    n = gram.shape[0]
    return pl.pallas_call(
        functools.partial(rotation_kernel, 2),
        out_shape=jax.ShapeDtypeStruct((n, n), jnp.float32),
        in_specs=[pl.BlockSpec(memory_space=pltpu.VMEM)],
        out_specs=pl.BlockSpec(memory_space=pltpu.VMEM),
        scratch_shapes=[
            pltpu.VMEM((n, 2 * n), jnp.float32),
            pltpu.VMEM((WIDE, WIDE), jnp.float32),
        ],
        compiler_params=pltpu.CompilerParams(vmem_limit_bytes=48 * 2**20),
    )(gram)


def gram_of(cols_here):
    return lax.dot_general(
        cols_here,
        cols_here,
        (((0,), (0,)), ((), ())),
        precision=HIGH,
        preferred_element_type=jnp.float32,
    )


def pack_kernel(order_ref, src_ref, dst_ref, sem):
    copies = [
        pltpu.make_async_copy(
            src_ref.at[:, pl.ds(pl.multiple_of(order_ref[i] * BLK, BLK), BLK)],
            dst_ref.at[i // 2, :, pl.ds(i % 2 * BLK, BLK)],
            sem.at[i],
        )
        for i in range(order_ref.shape[0])
    ]
    for copy in copies:
        copy.start()
    for copy in copies:
        copy.wait()


def unpack_kernel(order_ref, src_ref, dst_ref, sem):
    copies = [
        pltpu.make_async_copy(
            src_ref.at[i // 2, :, pl.ds(i % 2 * BLK, BLK)],
            dst_ref.at[:, pl.ds(pl.multiple_of(order_ref[i] * BLK, BLK), BLK)],
            sem.at[i],
        )
        for i in range(order_ref.shape[0])
    ]
    for copy in copies:
        copy.start()
    for copy in copies:
        copy.wait()


def move_blocks(kernel, array, order, shape):
    return pl.pallas_call(
        kernel,
        out_shape=jax.ShapeDtypeStruct(shape, jnp.float32),
        in_specs=[
            pl.BlockSpec(memory_space=pltpu.SMEM),
            pl.BlockSpec(memory_space=pl.ANY),
        ],
        out_specs=pl.BlockSpec(memory_space=pl.ANY),
        scratch_shapes=[pltpu.SemaphoreType.DMA((order.shape[0],))],
    )(order, array)


def pack_blocks(matrix, order):
    rows, width = matrix.shape
    return move_blocks(pack_kernel, matrix, order, (width // (2 * BLK), rows, 2 * BLK))


def unpack_blocks(packed, order):
    pairs, rows, span = packed.shape
    return move_blocks(unpack_kernel, packed, order, (rows, pairs * span))


def pair_places(count):
    half = count // 2
    return [2 * k if k < half else 2 * (count - 1 - k) + 1 for k in range(count)]


def pair_round(owned_pair):
    turn = rotation_of(lax.psum(gram_of(owned_pair), "rows"))
    return mul(owned_pair, turn, ((1,), (1,)))


def exchange(chunks):
    return lax.all_to_all(chunks, "cols", split_axis=0, concat_axis=0, tiled=True)


def make_body(count):
    places = pair_places(count)
    pair_at = np.argsort(np.array(places))
    slots = np.stack([2 * pair_at, 2 * pair_at + 1], axis=1).reshape(-1)
    ring = [(places[k], places[(k + 1) % count]) for k in range(count)]

    def body(upper, matching):
        rows = upper.shape[0]
        chunks = exchange(pack_blocks(upper, matching[0][slots]))
        owned = chunks.reshape(count * rows, 2 * BLK)
        owned = pair_round(owned)
        second = lax.ppermute(owned[:, BLK:], "cols", ring)
        owned = jnp.concatenate([owned[:, :BLK], second], axis=1)
        owned = pair_round(owned)
        returned = exchange(owned.reshape(count, rows, 2 * BLK))
        return unpack_blocks(returned, matching[1][slots])

    return body


def solution(mesh):
    in_specs = (P(("rows", "cols"), None), P())
    out_specs = P(("rows", "cols"), None)
    return jax.shard_map(
        make_body(mesh.shape["cols"]),
        mesh=mesh,
        in_specs=in_specs,
        out_specs=out_specs,
        check_vma=False,
    )
```

time: 778 us -> 476 us (0.61)
  other arithmetic: 402 us -> 0.66 us
  Pallas kernels: 20.3 us -> 226 us
  matrix products: 87.4 us -> 20.9 us
  local copies, waits for them, and re-layouts: 41.9 us -> 7.21 us
    another operation x80 -> x0, other arithmetic: 392 us -> none  [the longest x48 208 us: blocked_cholesky(): diag_part = jnp.linalg.cholesky(trailing[:width, :width])]
    pallas_call x2 -> x4, Pallas kernels: 20.3 us -> 226 us  [the longest x2 131 us: move_blocks(): pl.pallas_call(kernel, out_shape=jax.ShapeDtypeStruct(shape, jnp.float32)...]
    dot_general x28 -> x2, matrix products: 45.1 us -> 11.8 us  [mul(): lax.dot_general(a, b, (dims, ((), ())), precision=HIGH, preferred_element...]
    another operation x28 -> x0, matrix products: 22.4 us -> none  [the longest x16 12.7 us: apply_inverse(): jax.scipy.linalg.solve_triangular(diag_part, right_side.T, lower=True)]
    unnamed x100 -> x6, local copies, waits for them, and re-layouts: 15.3 us -> 3.79 us
    dot_general x6 -> x2, matrix products: 19.9 us -> 9.13 us  [gram_of(): lax.dot_general(cols_here, cols_here, (((0,), (0,)), ((), ())), precision...]
    div x16 -> x0, other arithmetic: 9.65 us -> none  [blocked_cholesky(): diag_part = jnp.linalg.cholesky(trailing[:width, :width])]
    select_n x12 -> x0, local copies, waits for them, and re-layouts: 9.28 us -> none  [blocked_cholesky(): diag_part = jnp.linalg.cholesky(trailing[:width, :width])]
where the time goes in v2:
time: 476 us; the launch traced here: 472 us
  Pallas kernels  226 us (47%)
  waiting for transfers between devices  141 us (30%)
  blocking collectives  55.5 us (12%)
  matrix products  20.9 us (4%)
  between operations  13.7 us (3%)
  starting transfers between devices  7.62 us (2%)
  local copies, waits for them, and re-layouts  7.21 us (2%)
    pallas_call x2, Pallas kernels, move_blocks(): pl.pallas_call(kernel, out_shape=jax.ShapeDtypeStruct(shape, jnp.float32)...  131 us
    pallas_call x2, Pallas kernels, rotation_of(): pl.pallas_call(functools.partial(rotation_kernel, 2), out_shape=jax.Shape...  94.7 us
    psum x2, waiting for transfers between devices, pair_round(): turn = rotation_of(lax.psum(gram_of(owned_pair), 'rows'))  71.4 us
    all_to_all x1, blocking collectives, exchange(): lax.all_to_all(chunks, 'cols', split_axis=0, concat_axis=0, tiled=True)  55.5 us
    all_to_all x1, waiting for transfers between devices, exchange(): lax.all_to_all(chunks, 'cols', split_axis=0, concat_axis=0, tiled=True)  46.5 us
    ppermute x1, waiting for transfers between devices, body(): second = lax.ppermute(owned[:, BLK:], 'cols', ring)  23.2 us
    dot_general x2, matrix products, mul(): lax.dot_general(a, b, (dims, ((), ())), precision=HIGH, preferred_element...  11.8 us
  transfers between devices with their start and end apart: 4, of which 4 were waited for; matrix products, arithmetic and copies ran while one was open for 0% of the time, Pallas kernels for 0%

profile of v2, /device:TPU:0, one launch (start us, length us, event | category | flops | bytes accessed | tf_op | source)
XLA Modules:
  0.0 472.4 jit_solution(15546738290099770645)
XLA Ops:
  6.5 0.0 all-reduce.3.cloned.1.call-start
  6.5 0.8 slice_bitcast_fusion
  7.3 0.7 pad_clamp_fusion
  8.0 1.2 gather_fusion.1
  9.2 65.4 %shard_map.55 = f32[8,128,512]{2,1,0:T(8,128)} custom-call(s32[16]{0:T(128)} %gather_fusion.1, f32[128,4096]{1,0:T(8,128)} %src_ref.1), custom_call_target="tpu_custom_call" | custom-call | tf_op jit(solution)/shard_map/pallas_call | solution.py:160
  74.6 55.5 %all_to_all.10 = f32[8,128,512]{2,1,0:T(8,128)S(1)} all-to-all(f32[8,128,512]{2,1,0:T(8,128)} %shard_map.55), channel_id=1, replica_groups=mesh['rows'=4,'cols'=8] {'cols'}, dimensions={0} | all-to-all | bytes 4194304 | tf_op jit(solution)/shard_map/all_to_all | solution.py:193
  130.2 4.6 convolution_bitcast_fusion
  134.8 0.0 all-reduce.3.cloned.1.call-update
  134.8 0.6 all-reduce.5.cloned.1.call-start
  135.4 34.7 %all-reduce.3.cloned.1.call-done.gram_ref = f32[512,512]{1,0:T(8,128)} async-done(((f32[512,512]{1,0:T(8,128)}), f32[512,512]{1,0:T(8,128)}) %all-reduce.3.cloned.1.call-update) | async-done | bytes 1048592 | tf_op jit(solution)/shard_map/psum | solution.py:188
  170.1 0.0 copy-start
  170.1 1.2 copy-done
  171.3 47.2 %shard_map.56 = f32[512,512]{1,0:T(8,128)S(1)} custom-call(f32[512,512]{1,0:T(8,128)S(1)} %copy-done), custom_call_target="tpu_custom_call" | custom-call | tf_op jit(solution)/shard_map/pallas_call | solution.py:106
  218.5 3.5 fusion.5
  222.1 0.2 fusion.4
  222.3 1.5 collective-permute-start
  223.8 23.2 %collective-permute-done = f32[1024,256]{0,1:T(8,128)S(1)} collective-permute-done((f32[1024,256]{0,1:T(8,128)S(1)}, f32[1024,256]{0,1:T(8,128)S(1)}, u32[]{:S(2)}, u32[]{:S(2)}) %collective-permute-start) | collective-permute-done | bytes 1048608 | tf_op jit(solution)/shard_map/ppermute | solution.py:207
  247.0 4.5 fusion.1
  251.5 0.0 all-reduce.5.cloned.1.call-update
  251.5 36.7 %all-reduce.5.cloned.1.call-done.gram_ref = f32[512,512]{1,0:T(8,128)} async-done(((f32[512,512]{1,0:T(8,128)}), f32[512,512]{1,0:T(8,128)}) %all-reduce.5.cloned.1.call-update) | async-done | bytes 1048592 | tf_op jit(solution)/shard_map/psum | solution.py:188
  288.3 0.0 copy-start.1
  288.3 1.2 copy-done.1
  289.5 47.5 %shard_map.57 = f32[512,512]{1,0:T(8,128)S(1)} custom-call(f32[512,512]{1,0:T(8,128)S(1)} %copy-done.1), custom_call_target="tpu_custom_call" | custom-call | tf_op jit(solution)/shard_map/pallas_call | solution.py:106
  337.0 8.2 %fusion = f32[1024,512]{1,0:T(8,128)} fusion(f32[512,512]{1,0:T(8,128)S(1)} %shard_map.57, f32[1024,256]{0,1:T(8,128)S(1)} %collective-permute-done, f32[1024,256]{0,1:T(8,128)S(1)} %get-tuple-element.5), kind=kOutput, calls=%fused_computation.3 | convolution fusion | flops 3221749760 | bytes 5242880 | tf_op jit(solution)/shard_map/dot_general | solution.py:62
  345.2 5.5 %all-to-all-start.1 = ((f32[8,128,512]{2,1,0:T(8,128)}), f32[8,128,512]{2,1,0:T(8,128)S(1)}, u32[]{:S(2)}, u32[]{:S(2)}) async-start(f32[8,128,512]{2,1,0:T(8,128)} %bitcast.14), calls=%async_computation.1 | async-start | bytes 4194304 | tf_op jit(solution)/shard_map/all_to_all | solution.py:193
  350.7 1.2 gather_fusion
  351.9 46.5 %all-to-all-done.1.src_ref = f32[8,128,512]{2,1,0:T(8,128)S(1)} async-done(((f32[8,128,512]{2,1,0:T(8,128)}), f32[8,128,512]{2,1,0:T(8,128)S(1)}, u32[]{:S(2)}, u32[]{:S(2)}) %all-to-all-start.1) | async-done | bytes 2097184 | tf_op jit(solution)/shard_map/all_to_all | solution.py:193
  398.5 0.0 copy-start.2
  398.5 1.3 copy-done.2
  399.8 65.4 %shard_map.58 = f32[128,4096]{1,0:T(8,128)} custom-call(s32[16]{0:T(128)} %gather_fusion, f32[8,128,512]{2,1,0:T(8,128)} %copy-done.2), custom_call_target="tpu_custom_call" | custom-call | tf_op jit(solution)/shard_map/pallas_call | solution.py:160
Async XLA Ops:
  6.5 163.5 %all-reduce.3.cloned.1.call-start = ((), (), s32[]{:S(2)}) async-start(), calls=%async_computation.2 | async-start | bytes 2097152 | tf_op jit(solution)/shard_map/psum | solution.py:188
  134.8 153.4 %all-reduce.5.cloned.1.call-start = ((), (), s32[]{:S(2)}) async-start(), calls=%async_computation.3 | async-start | bytes 2097152 | tf_op jit(solution)/shard_map/psum | solution.py:188
  170.1 1.2 copy-start
  222.3 24.7 %collective-permute-start = (f32[1024,256]{0,1:T(8,128)S(1)}, f32[1024,256]{0,1:T(8,128)S(1)}, u32[]{:S(2)}, u32[]{:S(2)}) collective-permute-start(f32[1024,256]{0,1:T(8,128)S(1)} %get-tuple-element.6), channel_id=1, source_target_pairs={{0,2},{2,4},{4,6},{6,7},{7,5},{5,3},{3,1},{1,0},{8,10},{10,12},{12... | collective-permute-start | bytes 3145736 | tf_op jit(solution)/shard_map/ppermute | solution.py:207
  288.3 1.2 copy-start.1
  345.2 53.3 %all-to-all-start.1 = ((f32[8,128,512]{2,1,0:T(8,128)}), f32[8,128,512]{2,1,0:T(8,128)S(1)}, u32[]{:S(2)}, u32[]{:S(2)}) async-start(f32[8,128,512]{2,1,0:T(8,128)} %bitcast.14), calls=%async_computation.1 | async-start | bytes 4194304 | tf_op jit(solution)/shard_map/all_to_all | solution.py:193
  398.5 1.3 copy-start.2
Sparse Core Ops, SparseCore 0:
  134.9 35.0 all-reduce.2
  251.6 36.5 all-reduce.4

commit v3 on v2

--- a/solution.py
+++ b/solution.py
@@ -126,34 +126,16 @@
     )
 
 
-def pack_kernel(order_ref, src_ref, dst_ref, sem):
-    copies = [
-        pltpu.make_async_copy(
-            src_ref.at[:, pl.ds(pl.multiple_of(order_ref[i] * BLK, BLK), BLK)],
-            dst_ref.at[i // 2, :, pl.ds(i % 2 * BLK, BLK)],
-            sem.at[i],
-        )
-        for i in range(order_ref.shape[0])
-    ]
-    for copy in copies:
-        copy.start()
-    for copy in copies:
-        copy.wait()
-
-
-def unpack_kernel(order_ref, src_ref, dst_ref, sem):
-    copies = [
-        pltpu.make_async_copy(
-            src_ref.at[i // 2, :, pl.ds(i % 2 * BLK, BLK)],
-            dst_ref.at[:, pl.ds(pl.multiple_of(order_ref[i] * BLK, BLK), BLK)],
-            sem.at[i],
-        )
-        for i in range(order_ref.shape[0])
-    ]
-    for copy in copies:
-        copy.start()
-    for copy in copies:
-        copy.wait()
+def pack_kernel(order_ref, src_ref, dst_ref):
+    for i in range(order_ref.shape[0]):
+        at = pl.ds(pl.multiple_of(order_ref[i] * BLK, BLK), BLK)
+        dst_ref[i // 2, :, pl.ds(i % 2 * BLK, BLK)] = src_ref[:, at]
+
+
+def unpack_kernel(order_ref, src_ref, dst_ref):
+    for i in range(order_ref.shape[0]):
+        at = pl.ds(pl.multiple_of(order_ref[i] * BLK, BLK), BLK)
+        dst_ref[:, at] = src_ref[i // 2, :, pl.ds(i % 2 * BLK, BLK)]
 
 
 def move_blocks(kernel, array, order, shape):
@@ -162,10 +144,10 @@
         out_shape=jax.ShapeDtypeStruct(shape, jnp.float32),
         in_specs=[
             pl.BlockSpec(memory_space=pltpu.SMEM),
-            pl.BlockSpec(memory_space=pl.ANY),
+            pl.BlockSpec(memory_space=pltpu.VMEM),
         ],
-        out_specs=pl.BlockSpec(memory_space=pl.ANY),
-        scratch_shapes=[pltpu.SemaphoreType.DMA((order.shape[0],))],
+        out_specs=pl.BlockSpec(memory_space=pltpu.VMEM),
+        compiler_params=pltpu.CompilerParams(vmem_limit_bytes=48 * 2**20),
     )(order, array)
 
 
@@ -179,47 +161,50 @@
     return move_blocks(unpack_kernel, packed, order, (rows, pairs * span))
 
 
-def pair_places(count):
-    half = count // 2
-    return [2 * k if k < half else 2 * (count - 1 - k) + 1 for k in range(count)]
+def pair_places(rows, low):
+    path = [0, 1, 3, 2] if rows == 4 else list(range(rows))
+    places = []
+    for at in range(low):
+        places += [r * low + at for r in (path if at % 2 == 0 else path[::-1])]
+    return places
+
+
+GROUP = ("rows", "low")
 
 
 def pair_round(owned_pair):
-    turn = rotation_of(lax.psum(gram_of(owned_pair), "rows"))
+    turn = rotation_of(lax.psum(gram_of(owned_pair), "high"))
     return mul(owned_pair, turn, ((1,), (1,)))
 
 
 def exchange(chunks):
-    return lax.all_to_all(chunks, "cols", split_axis=0, concat_axis=0, tiled=True)
-
-
-def make_body(count):
-    places = pair_places(count)
+    return lax.all_to_all(chunks, GROUP, split_axis=0, concat_axis=0, tiled=True)
+
+
+def make_body(rows, low):
+    count = rows * low
+    places = pair_places(rows, low)
     pair_at = np.argsort(np.array(places))
     slots = np.stack([2 * pair_at, 2 * pair_at + 1], axis=1).reshape(-1)
     ring = [(places[k], places[(k + 1) % count]) for k in range(count)]
 
     def body(upper, matching):
-        rows = upper.shape[0]
+        deep = upper.shape[0]
         chunks = exchange(pack_blocks(upper, matching[0][slots]))
-        owned = chunks.reshape(count * rows, 2 * BLK)
-        owned = pair_round(owned)
-        second = lax.ppermute(owned[:, BLK:], "cols", ring)
-        owned = jnp.concatenate([owned[:, :BLK], second], axis=1)
-        owned = pair_round(owned)
-        returned = exchange(owned.reshape(count, rows, 2 * BLK))
+        owned = pair_round(chunks.reshape(count * deep, 2 * BLK))
+        second = lax.ppermute(owned[:, BLK:], GROUP, ring)
+        owned = pair_round(jnp.concatenate([owned[:, :BLK], second], axis=1))
+        returned = exchange(owned.reshape(count, deep, 2 * BLK))
         return unpack_blocks(returned, matching[1][slots])
 
     return body
 
 
 def solution(mesh):
-    in_specs = (P(("rows", "cols"), None), P())
-    out_specs = P(("rows", "cols"), None)
+    rows, cols = mesh.shape["rows"], mesh.shape["cols"]
+    low = cols // rows
+    split = jax.sharding.Mesh(mesh.devices.reshape(rows, cols // low, low), ("rows", "high", "low"))
+    spec = P(("rows", "high", "low"), None)
     return jax.shard_map(
-        make_body(mesh.shape["cols"]),
-        mesh=mesh,
-        in_specs=in_specs,
-        out_specs=out_specs,
-        check_vma=False,
+        make_body(rows, low), mesh=split, in_specs=(spec, P()), out_specs=spec, check_vma=False
     )

time: 476 us -> 321 us (0.67)
  Pallas kernels: 226 us -> 97.4 us
  blocking collectives: 55.5 us -> 30.7 us
    pallas_call x2, Pallas kernels: 131 us -> 2.71 us  [move_blocks(): pl.pallas_call(kernel, out_shape=jax.ShapeDtypeStruct(shape, jnp.float32)...]
    psum x2, waiting for transfers between devices: 71.4 us -> 103 us  [pair_round(): turn = rotation_of(lax.psum(gram_of(owned_pair), 'high'))]
    all_to_all x1, blocking collectives: 55.5 us -> 30.7 us  [exchange(): lax.all_to_all(chunks, GROUP, split_axis=0, concat_axis=0, tiled=True)]
    all_to_all x1, waiting for transfers between devices: 46.5 us -> 25.1 us  [exchange(): lax.all_to_all(chunks, GROUP, split_axis=0, concat_axis=0, tiled=True)]
    ppermute x1, waiting for transfers between devices: 23.2 us -> 14.8 us  [body(): second = lax.ppermute(owned[:, BLK:], GROUP, ring)]
where the time goes in v3:
time: 321 us; the launch traced here: 317 us
  waiting for transfers between devices  143 us (45%)
  Pallas kernels  97.4 us (30%)
  blocking collectives  30.7 us (10%)
  matrix products  20.9 us (7%)
  between operations  13.7 us (4%)
  local copies, waits for them, and re-layouts  6.3 us (2%)
  starting transfers between devices  4.34 us (1%)
    psum x2, waiting for transfers between devices, pair_round(): turn = rotation_of(lax.psum(gram_of(owned_pair), 'high'))  103 us
    pallas_call x2, Pallas kernels, rotation_of(): pl.pallas_call(functools.partial(rotation_kernel, 2), out_shape=jax.Shape...  94.7 us
    all_to_all x1, blocking collectives, exchange(): lax.all_to_all(chunks, GROUP, split_axis=0, concat_axis=0, tiled=True)  30.7 us
    all_to_all x1, waiting for transfers between devices, exchange(): lax.all_to_all(chunks, GROUP, split_axis=0, concat_axis=0, tiled=True)  25.1 us
    ppermute x1, waiting for transfers between devices, body(): second = lax.ppermute(owned[:, BLK:], GROUP, ring)  14.8 us
    dot_general x2, matrix products, mul(): lax.dot_general(a, b, (dims, ((), ())), precision=HIGH, preferred_element...  11.8 us
    dot_general x2, matrix products, gram_of(): lax.dot_general(cols_here, cols_here, (((0,), (0,)), ((), ())), precision...  9.13 us
  transfers between devices with their start and end apart: 4, of which 4 were waited for; matrix products, arithmetic and copies ran while one was open for 0% of the time, Pallas kernels for 0%

profile of v3, /device:TPU:0, one launch (start us, length us, event | category | flops | bytes accessed | tf_op | source)
XLA Modules:
  0.0 316.9 jit_solution(14537597635468872621)
XLA Ops:
  6.5 0.0 all-reduce.3.cloned.1.call-start
  6.5 0.8 slice_bitcast_fusion
  7.3 0.7 pad_clamp_fusion
  8.0 0.7 gather_fusion.1
  8.6 0.0 copy-start
  8.6 1.6 copy-done
  10.2 0.7 shard_map.55
  10.9 30.7 %all_to_all.10 = f32[8,128,512]{2,1,0:T(8,128)S(1)} all-to-all(f32[8,128,512]{2,1,0:T(8,128)S(1)} %shard_map.55), channel_id=1, replica_groups=mesh['rows'=4,'high'=4,'low'=2] {'rows','low'}, dimensions={0} | all-to-all | bytes 4194304 | tf_op jit(solution)/shard_map/all_to_all | solution.py:181
  41.6 4.6 %convolution_bitcast_fusion = f32[512,512]{1,0:T(8,128)} fusion(f32[8,128,512]{2,1,0:T(8,128)S(1)} %all_to_all.10), kind=kOutput, calls=%fused_computation.5 | convolution fusion | flops 3221225472 | bytes 3145728 | tf_op jit(solution)/shard_map/dot_general | solution.py:120
  46.2 0.0 all-reduce.3.cloned.1.call-update
  46.2 0.6 all-reduce.5.cloned.1.call-start
  46.8 51.7 %all-reduce.3.cloned.1.call-done.gram_ref = f32[512,512]{1,0:T(8,128)} async-done(((f32[512,512]{1,0:T(8,128)}), f32[512,512]{1,0:T(8,128)}) %all-reduce.3.cloned.1.call-update) | async-done | bytes 1048592 | tf_op jit(solution)/shard_map/psum | solution.py:176
  98.5 0.0 copy-start.1
  98.5 1.2 copy-done.1
  99.7 47.2 %shard_map.56 = f32[512,512]{1,0:T(8,128)S(1)} custom-call(f32[512,512]{1,0:T(8,128)S(1)} %copy-done.1), custom_call_target="tpu_custom_call" | custom-call | tf_op jit(solution)/shard_map/pallas_call | solution.py:106
  146.9 3.5 %fusion.5 = f32[1024,512]{0,1:T(8,128)S(1)} fusion(f32[1024,512]{1,0:T(8,128)S(1)} %bitcast.13, f32[512,512]{1,0:T(8,128)S(1)} %shard_map.56), kind=kOutput, calls=%fused_computation.12 | convolution fusion | flops 3221225472 | bytes 5242880 | tf_op jit(solution)/shard_map/dot_general | solution.py:62
  150.5 0.2 fusion.4
  150.7 0.1 collective-permute-start
  150.8 14.8 %collective-permute-done = f32[1024,256]{0,1:T(8,128)S(1)} collective-permute-done((f32[1024,256]{0,1:T(8,128)S(1)}, f32[1024,256]{0,1:T(8,128)S(1)}, u32[]{:S(2)}, u32[]{:S(2)}) %collective-permute-start) | collective-permute-done | bytes 1048608 | tf_op jit(solution)/shard_map/ppermute | solution.py:195
  165.5 4.5 %fusion.1 = f32[512,512]{1,0:T(8,128)} fusion(f32[1024,256]{0,1:T(8,128)S(1)} %collective-permute-done, f32[1024,256]{0,1:T(8,128)S(1)} %get-tuple-element.5), kind=kOutput, calls=%fused_computation.4 | convolution fusion | flops 3221749760 | bytes 3145728 | tf_op jit(solution)/shard_map/dot_general | solution.py:120
  170.0 0.0 all-reduce.5.cloned.1.call-update
  170.1 51.4 %all-reduce.5.cloned.1.call-done.gram_ref = f32[512,512]{1,0:T(8,128)} async-done(((f32[512,512]{1,0:T(8,128)}), f32[512,512]{1,0:T(8,128)}) %all-reduce.5.cloned.1.call-update) | async-done | bytes 1048592 | tf_op jit(solution)/shard_map/psum | solution.py:176
  221.4 0.0 copy-start.2
  221.4 1.2 copy-done.2
  222.6 47.5 %shard_map.57 = f32[512,512]{1,0:T(8,128)S(1)} custom-call(f32[512,512]{1,0:T(8,128)S(1)} %copy-done.2), custom_call_target="tpu_custom_call" | custom-call | tf_op jit(solution)/shard_map/pallas_call | solution.py:106
  270.1 8.2 %fusion = f32[1024,512]{1,0:T(8,128)} fusion(f32[512,512]{1,0:T(8,128)S(1)} %shard_map.57, f32[1024,256]{0,1:T(8,128)S(1)} %collective-permute-done, f32[1024,256]{0,1:T(8,128)S(1)} %get-tuple-element.5), kind=kOutput, calls=%fused_computation.3 | convolution fusion | flops 3221749760 | bytes 5242880 | tf_op jit(solution)/shard_map/dot_general | solution.py:62
  278.3 3.7 %all-to-all-start.1 = ((f32[8,128,512]{2,1,0:T(8,128)}), f32[8,128,512]{2,1,0:T(8,128)S(1)}, u32[]{:S(2)}, u32[]{:S(2)}) async-start(f32[8,128,512]{2,1,0:T(8,128)} %bitcast.14), calls=%async_computation.1 | async-start | bytes 4194304 | tf_op jit(solution)/shard_map/all_to_all | solution.py:181
  282.0 0.7 gather_fusion
  282.6 25.1 %all-to-all-done.1.src_ref = f32[8,128,512]{2,1,0:T(8,128)S(1)} async-done(((f32[8,128,512]{2,1,0:T(8,128)}), f32[8,128,512]{2,1,0:T(8,128)S(1)}, u32[]{:S(2)}, u32[]{:S(2)}) %all-to-all-start.1) | async-done | bytes 2097184 | tf_op jit(solution)/shard_map/all_to_all | solution.py:181
  307.8 2.0 shard_map.58
Async XLA Ops:
  6.5 91.9 %all-reduce.3.cloned.1.call-start = ((), (), s32[]{:S(2)}) async-start(), calls=%async_computation.2 | async-start | bytes 2097152 | tf_op jit(solution)/shard_map/psum | solution.py:176
  8.6 1.6 copy-start
  46.2 175.2 %all-reduce.5.cloned.1.call-start = ((), (), s32[]{:S(2)}) async-start(), calls=%async_computation.3 | async-start | bytes 2097152 | tf_op jit(solution)/shard_map/psum | solution.py:176
  98.5 1.2 copy-start.1
  150.7 14.9 %collective-permute-start = (f32[1024,256]{0,1:T(8,128)S(1)}, f32[1024,256]{0,1:T(8,128)S(1)}, u32[]{:S(2)}, u32[]{:S(2)}) collective-permute-start(f32[1024,256]{0,1:T(8,128)S(1)} %get-tuple-element.6), channel_id=1, source_target_pairs={{0,8},{8,24},{24,16},{16,17},{17,25},{25,9},{9,1},{1,0},{2,10},{10... | collective-permute-start | bytes 3145736 | tf_op jit(solution)/shard_map/ppermute | solution.py:195
  221.4 1.2 copy-start.2
  278.3 29.4 %all-to-all-start.1 = ((f32[8,128,512]{2,1,0:T(8,128)}), f32[8,128,512]{2,1,0:T(8,128)S(1)}, u32[]{:S(2)}, u32[]{:S(2)}) async-start(f32[8,128,512]{2,1,0:T(8,128)} %bitcast.14), calls=%async_computation.1 | async-start | bytes 4194304 | tf_op jit(solution)/shard_map/all_to_all | solution.py:181
Sparse Core Ops, SparseCore 0:
  46.4 52.0 all-reduce.2
  170.2 51.1 all-reduce.4

commit v4 on v3

--- a/solution.py
+++ b/solution.py
@@ -126,6 +126,79 @@
     )
 
 
+def sum_kernel(peers, gram_ref, out_ref, mine, total, landed, sems):
+    tiles = gram_ref.shape[0] // WIDE
+    upper = [(i, j) for i in range(tiles) for j in range(i, tiles)]
+    share = len(upper) * WIDE // peers
+    me = lax.axis_index("high")
+    for t, (i, j) in enumerate(upper):
+        mine[t * WIDE : (t + 1) * WIDE, :] = gram_ref[
+            i * WIDE : (i + 1) * WIDE, j * WIDE : (j + 1) * WIDE
+        ]
+    others = [lax.rem(me + k, peers) for k in range(1, peers)]
+    barrier = pltpu.get_barrier_semaphore()
+    for other in others:
+        pl.semaphore_signal(
+            barrier, inc=1, device_id={"high": other}, device_id_type=pl.DeviceIdType.MESH
+        )
+    pl.semaphore_wait(barrier, peers - 1)
+
+    def part(who):
+        return pl.ds(pl.multiple_of(who * share, SUB), share)
+
+    def send(src, dst, phase, k):
+        return pltpu.make_async_remote_copy(
+            src_ref=src,
+            dst_ref=dst,
+            send_sem=sems.at[2 * phase, k],
+            recv_sem=sems.at[2 * phase + 1, k],
+            device_id={"high": others[k]},
+            device_id_type=pl.DeviceIdType.MESH,
+        )
+
+    scatter = [send(mine.at[part(others[k])], landed.at[k], 0, k) for k in range(peers - 1)]
+    for copy in scatter:
+        copy.start()
+    whole = mine[part(me), :]
+    for k, copy in enumerate(scatter):
+        copy.wait_recv()
+        whole = whole + landed[k]
+    total[part(me), :] = whole
+    gather = [send(total.at[part(me)], total.at[part(me)], 1, k) for k in range(peers - 1)]
+    for copy in gather:
+        copy.start()
+    for copy in scatter:
+        copy.wait_send()
+    for copy in gather:
+        copy.wait()
+    for t, (i, j) in enumerate(upper):
+        tile = total[t * WIDE : (t + 1) * WIDE, :]
+        out_ref[i * WIDE : (i + 1) * WIDE, j * WIDE : (j + 1) * WIDE] = tile
+        if j > i:
+            out_ref[j * WIDE : (j + 1) * WIDE, i * WIDE : (i + 1) * WIDE] = tile.T
+
+
+def summed(gram, peers):
+    n = gram.shape[0]
+    tiles = n // WIDE
+    deep = tiles * (tiles + 1) // 2 * WIDE
+    return pl.pallas_call(
+        functools.partial(sum_kernel, peers),
+        out_shape=jax.ShapeDtypeStruct((n, n), jnp.float32),
+        in_specs=[pl.BlockSpec(memory_space=pltpu.VMEM)],
+        out_specs=pl.BlockSpec(memory_space=pltpu.VMEM),
+        scratch_shapes=[
+            pltpu.VMEM((deep, WIDE), jnp.float32),
+            pltpu.VMEM((deep, WIDE), jnp.float32),
+            pltpu.VMEM((peers - 1, deep // peers, WIDE), jnp.float32),
+            pltpu.SemaphoreType.DMA((4, peers - 1)),
+        ],
+        compiler_params=pltpu.CompilerParams(
+            collective_id=0, has_side_effects=True, vmem_limit_bytes=32 * 2**20
+        ),
+    )(gram)
+
+
 def pack_kernel(order_ref, src_ref, dst_ref):
     for i in range(order_ref.shape[0]):
         at = pl.ds(pl.multiple_of(order_ref[i] * BLK, BLK), BLK)
@@ -172,8 +245,8 @@
 GROUP = ("rows", "low")
 
 
-def pair_round(owned_pair):
-    turn = rotation_of(lax.psum(gram_of(owned_pair), "high"))
+def pair_round(owned_pair, high):
+    turn = rotation_of(summed(gram_of(owned_pair), high))
     return mul(owned_pair, turn, ((1,), (1,)))
 
 
@@ -181,7 +254,7 @@
     return lax.all_to_all(chunks, GROUP, split_axis=0, concat_axis=0, tiled=True)
 
 
-def make_body(rows, low):
+def make_body(rows, high, low):
     count = rows * low
     places = pair_places(rows, low)
     pair_at = np.argsort(np.array(places))
@@ -191,9 +264,9 @@
     def body(upper, matching):
         deep = upper.shape[0]
         chunks = exchange(pack_blocks(upper, matching[0][slots]))
-        owned = pair_round(chunks.reshape(count * deep, 2 * BLK))
+        owned = pair_round(chunks.reshape(count * deep, 2 * BLK), high)
         second = lax.ppermute(owned[:, BLK:], GROUP, ring)
-        owned = pair_round(jnp.concatenate([owned[:, :BLK], second], axis=1))
+        owned = pair_round(jnp.concatenate([owned[:, :BLK], second], axis=1), high)
         returned = exchange(owned.reshape(count, deep, 2 * BLK))
         return unpack_blocks(returned, matching[1][slots])
 
@@ -203,8 +276,9 @@
 def solution(mesh):
     rows, cols = mesh.shape["rows"], mesh.shape["cols"]
     low = cols // rows
-    split = jax.sharding.Mesh(mesh.devices.reshape(rows, cols // low, low), ("rows", "high", "low"))
+    high = cols // low
+    split = jax.sharding.Mesh(mesh.devices.reshape(rows, high, low), ("rows", "high", "low"))
     spec = P(("rows", "high", "low"), None)
     return jax.shard_map(
-        make_body(rows, low), mesh=split, in_specs=(spec, P()), out_specs=spec, check_vma=False
+        make_body(rows, high, low), mesh=split, in_specs=(spec, P()), out_specs=spec, check_vma=False
     )

time: 321 us -> 264 us (0.82)
  the two profiles are of different devices: /device:TPU:0 before, /device:TPU:25 now
where the time goes in v4:
time: 264 us; the launch traced here: 260 us
  Pallas kernels  165 us (62%)
  waiting for transfers between devices  36.4 us (14%)
  blocking collectives  29.8 us (11%)
  matrix products  18.9 us (7%)
  starting transfers between devices  4.76 us (2%)
  local copies, waits for them, and re-layouts  3.84 us (1%)
    pallas_call x2, Pallas kernels, rotation_of(): pl.pallas_call(functools.partial(rotation_kernel, 2), out_shape=jax.Shape...  95.2 us
    pallas_call x2, Pallas kernels, summed(): pl.pallas_call(functools.partial(sum_kernel, peers), out_shape=jax.ShapeD...  67.1 us
    all_to_all x1, blocking collectives, exchange(): lax.all_to_all(chunks, GROUP, split_axis=0, concat_axis=0, tiled=True)  29.8 us
    all_to_all x1, waiting for transfers between devices, exchange(): lax.all_to_all(chunks, GROUP, split_axis=0, concat_axis=0, tiled=True)  24.6 us
    ppermute x1, waiting for transfers between devices, body(): second = lax.ppermute(owned[:, BLK:], GROUP, ring)  11.7 us
    dot_general x2, matrix products, mul(): lax.dot_general(a, b, (dims, ((), ())), precision=HIGH, preferred_element...  11.7 us
    dot_general x2, matrix products, gram_of(): lax.dot_general(cols_here, cols_here, (((0,), (0,)), ((), ())), precision...  7.18 us
  transfers between devices with their start and end apart: 2, of which 2 were waited for; matrix products, arithmetic and copies ran while one was open for 0% of the time, Pallas kernels for 0%

profile of v4, /device:TPU:25, one launch (start us, length us, event | category | flops | bytes accessed | tf_op | source)
XLA Modules:
  0.0 259.7 jit_solution(2820267988638515216)
XLA Ops:
  0.0 0.8 slice_bitcast_fusion
  0.8 0.7 pad_clamp_fusion
  1.4 0.7 gather_fusion.1
  2.1 0.0 copy-start
  2.1 1.6 copy-done
  3.7 0.7 shard_map.55
  4.4 29.8 %all_to_all.10 = f32[8,128,512]{2,1,0:T(8,128)S(1)} all-to-all(f32[8,128,512]{2,1,0:T(8,128)S(1)} %shard_map.55), channel_id=1, replica_groups=mesh['rows'=4,'high'=4,'low'=2] {'rows','low'}, dimensions={0} | all-to-all | bytes 4194304 | tf_op jit(solution)/shard_map/all_to_all | solution.py:254
  34.1 3.6 %convolution_bitcast_fusion.gram_ref = f32[512,512]{1,0:T(8,128)S(1)} fusion(f32[8,128,512]{2,1,0:T(8,128)S(1)} %all_to_all.10), kind=kOutput, calls=%fused_computation.5 | convolution fusion | flops 3221225472 | bytes 3145728 | tf_op jit(solution)/shard_map/dot_general | solution.py:120
  37.8 33.0 %shard_map.56.gram_ref = f32[512,512]{1,0:T(8,128)S(1)} custom-call(f32[512,512]{1,0:T(8,128)S(1)} %convolution_bitcast_fusion.gram_ref), custom_call_target="tpu_custom_call" | custom-call | tf_op jit(solution)/shard_map/pallas_call | solution.py:185
  70.8 47.7 %shard_map.57 = f32[512,512]{1,0:T(8,128)S(1)} custom-call(f32[512,512]{1,0:T(8,128)S(1)} %shard_map.56.gram_ref), custom_call_target="tpu_custom_call" | custom-call | tf_op jit(solution)/shard_map/pallas_call | solution.py:106
  118.6 3.5 %fusion.5 = f32[1024,512]{0,1:T(8,128)S(1)} fusion(f32[1024,512]{1,0:T(8,128)S(1)} %bitcast.13, f32[512,512]{1,0:T(8,128)S(1)} %shard_map.57), kind=kOutput, calls=%fused_computation.12 | convolution fusion | flops 3221225472 | bytes 5242880 | tf_op jit(solution)/shard_map/dot_general | solution.py:62
  122.1 0.2 fusion.4
  122.3 0.8 collective-permute-start
  123.1 11.7 %collective-permute-done = f32[1024,256]{0,1:T(8,128)S(1)} collective-permute-done((f32[1024,256]{0,1:T(8,128)S(1)}, f32[1024,256]{0,1:T(8,128)S(1)}, u32[]{:S(2)}, u32[]{:S(2)}) %collective-permute-start) | collective-permute-done | bytes 1048608 | tf_op jit(solution)/shard_map/ppermute | solution.py:268
  134.8 3.5 %fusion.1.gram_ref = f32[512,512]{1,0:T(8,128)S(1)} fusion(f32[1024,256]{0,1:T(8,128)S(1)} %collective-permute-done, f32[1024,256]{0,1:T(8,128)S(1)} %get-tuple-element.5), kind=kOutput, calls=%fused_computation.4 | convolution fusion | flops 3221749760 | bytes 3145728 | tf_op jit(solution)/shard_map/dot_general | solution.py:120
  138.3 34.1 %shard_map.58.gram_ref = f32[512,512]{1,0:T(8,128)S(1)} custom-call(f32[512,512]{1,0:T(8,128)S(1)} %fusion.1.gram_ref), custom_call_target="tpu_custom_call" | custom-call | tf_op jit(solution)/shard_map/pallas_call | solution.py:185
  172.4 47.5 %shard_map.59 = f32[512,512]{1,0:T(8,128)S(1)} custom-call(f32[512,512]{1,0:T(8,128)S(1)} %shard_map.58.gram_ref), custom_call_target="tpu_custom_call" | custom-call | tf_op jit(solution)/shard_map/pallas_call | solution.py:106
  219.9 8.2 %fusion = f32[1024,512]{1,0:T(8,128)} fusion(f32[512,512]{1,0:T(8,128)S(1)} %shard_map.59, f32[1024,256]{0,1:T(8,128)S(1)} %collective-permute-done, f32[1024,256]{0,1:T(8,128)S(1)} %get-tuple-element.5), kind=kOutput, calls=%fused_computation.3 | convolution fusion | flops 3221749760 | bytes 5242880 | tf_op jit(solution)/shard_map/dot_general | solution.py:62
  228.1 4.0 %all-to-all-start.1 = ((f32[8,128,512]{2,1,0:T(8,128)}), f32[8,128,512]{2,1,0:T(8,128)S(1)}, u32[]{:S(2)}, u32[]{:S(2)}) async-start(f32[8,128,512]{2,1,0:T(8,128)} %bitcast.14), calls=%async_computation.1 | async-start | bytes 4194304 | tf_op jit(solution)/shard_map/all_to_all | solution.py:254
  232.1 0.7 gather_fusion
  232.8 24.6 %all-to-all-done.1.src_ref = f32[8,128,512]{2,1,0:T(8,128)S(1)} async-done(((f32[8,128,512]{2,1,0:T(8,128)}), f32[8,128,512]{2,1,0:T(8,128)S(1)}, u32[]{:S(2)}, u32[]{:S(2)}) %all-to-all-start.1) | async-done | bytes 2097184 | tf_op jit(solution)/shard_map/all_to_all | solution.py:254
  257.4 2.0 shard_map.60
Async XLA Ops:
  2.1 1.6 copy-start
  122.3 12.5 %collective-permute-start = (f32[1024,256]{0,1:T(8,128)S(1)}, f32[1024,256]{0,1:T(8,128)S(1)}, u32[]{:S(2)}, u32[]{:S(2)}) collective-permute-start(f32[1024,256]{0,1:T(8,128)S(1)} %get-tuple-element.6), channel_id=1, source_target_pairs={{0,8},{8,24},{24,16},{16,17},{17,25},{25,9},{9,1},{1,0},{2,10},{10... | collective-permute-start | bytes 3145736 | tf_op jit(solution)/shard_map/ppermute | solution.py:268
  228.1 29.3 %all-to-all-start.1 = ((f32[8,128,512]{2,1,0:T(8,128)}), f32[8,128,512]{2,1,0:T(8,128)S(1)}, u32[]{:S(2)}, u32[]{:S(2)}) async-start(f32[8,128,512]{2,1,0:T(8,128)} %bitcast.14), calls=%async_computation.1 | async-start | bytes 4194304 | tf_op jit(solution)/shard_map/all_to_all | solution.py:254

commit v5 on v4

--- a/solution.py
+++ b/solution.py
@@ -234,6 +234,109 @@
     return move_blocks(unpack_kernel, packed, order, (rows, pairs * span))
 
 
+def in_group(low):
+    me = lax.axis_index("rows") * low + lax.axis_index("low")
+    return me, lambda at: {"rows": at // low, "low": at % low}
+
+
+def greet(count, me, where):
+    barrier = pltpu.get_barrier_semaphore()
+
+    def signal(k, carry):
+        pl.semaphore_signal(
+            barrier,
+            inc=1,
+            device_id=where((me + k) % count),
+            device_id_type=pl.DeviceIdType.MESH,
+        )
+        return carry
+
+    lax.fori_loop(1, count, signal, 0)
+    pl.semaphore_wait(barrier, count - 1)
+
+
+def chunk_copy(src, dst, sems, k, me, count, where):
+    at = (me + k) % count
+    return pltpu.make_async_remote_copy(
+        src_ref=src.at[at],
+        dst_ref=dst.at[me],
+        send_sem=sems.at[0, k],
+        recv_sem=sems.at[1, k],
+        device_id=where(at),
+        device_id_type=pl.DeviceIdType.MESH,
+    )
+
+
+def spread_kernel(low, packed, out_ref, sems):
+    count = out_ref.shape[0]
+    me, where = in_group(low)
+    greet(count, me, where)
+
+    def start(k, carry):
+        chunk_copy(packed, out_ref, sems, k, me, count, where).start()
+        return carry
+
+    def wait(k, carry):
+        chunk_copy(packed, out_ref, sems, k, me, count, where).wait()
+        return carry
+
+    lax.fori_loop(1, count, start, 0)
+    out_ref[me] = packed[me]
+    lax.fori_loop(1, count, wait, 0)
+
+
+def spread(packed, low):
+    return pl.pallas_call(
+        functools.partial(spread_kernel, low),
+        out_shape=jax.ShapeDtypeStruct(packed.shape, jnp.float32),
+        in_specs=[pl.BlockSpec(memory_space=pltpu.VMEM)],
+        out_specs=pl.BlockSpec(memory_space=pltpu.VMEM),
+        scratch_shapes=[pltpu.SemaphoreType.DMA((2, packed.shape[0]))],
+        compiler_params=pltpu.CompilerParams(
+            collective_id=1, has_side_effects=True, vmem_limit_bytes=48 * 2**20
+        ),
+    )(packed)
+
+
+def return_kernel(low, cols_ref, turn_ref, landed, turned, sems):
+    count = cols_ref.shape[0]
+    me, where = in_group(low)
+    greet(count, me, where)
+
+    def start(k, carry):
+        at = (me + k) % count
+        turned[at] = mul(cols_ref[at], turn_ref[...], ((1,), (1,)))
+        chunk_copy(turned, landed, sems, k, me, count, where).start()
+        return carry
+
+    def wait(k, carry):
+        chunk_copy(turned, landed, sems, k, me, count, where).wait()
+        return carry
+
+    lax.fori_loop(1, count, start, 0)
+    landed[me] = mul(cols_ref[me], turn_ref[...], ((1,), (1,)))
+    lax.fori_loop(1, count, wait, 0)
+
+
+def turn_back(owned, turn, low):
+    return pl.pallas_call(
+        functools.partial(return_kernel, low),
+        out_shape=jax.ShapeDtypeStruct(owned.shape, jnp.float32),
+        in_specs=[
+            pl.BlockSpec(memory_space=pltpu.VMEM),
+            pl.BlockSpec(memory_space=pltpu.VMEM),
+        ],
+        out_specs=pl.BlockSpec(memory_space=pltpu.VMEM),
+        scratch_shapes=[
+            pltpu.VMEM(owned.shape, jnp.float32),
+            pltpu.SemaphoreType.DMA((2, owned.shape[0])),
+        ],
+        compiler_params=pltpu.CompilerParams(
+            collective_id=2, has_side_effects=True, vmem_limit_bytes=48 * 2**20
+        ),
+    )(owned, turn)
+
+
 def pair_places(rows, low):
     path = [0, 1, 3, 2] if rows == 4 else list(range(rows))
     places = []
@@ -245,13 +348,8 @@
 GROUP = ("rows", "low")
 
 
-def pair_round(owned_pair, high):
-    turn = rotation_of(summed(gram_of(owned_pair), high))
-    return mul(owned_pair, turn, ((1,), (1,)))
-
-
-def exchange(chunks):
-    return lax.all_to_all(chunks, GROUP, split_axis=0, concat_axis=0, tiled=True)
+def turn_of(owned_pair, high):
+    return rotation_of(summed(gram_of(owned_pair), high))
 
 
 def make_body(rows, high, low):
@@ -263,11 +361,13 @@
 
     def body(upper, matching):
         deep = upper.shape[0]
-        chunks = exchange(pack_blocks(upper, matching[0][slots]))
-        owned = pair_round(chunks.reshape(count * deep, 2 * BLK), high)
+        chunks = spread(pack_blocks(upper, matching[0][slots]), low)
+        owned = chunks.reshape(count * deep, 2 * BLK)
+        owned = mul(owned, turn_of(owned, high), ((1,), (1,)))
         second = lax.ppermute(owned[:, BLK:], GROUP, ring)
-        owned = pair_round(jnp.concatenate([owned[:, :BLK], second], axis=1), high)
-        returned = exchange(owned.reshape(count, deep, 2 * BLK))
+        owned = jnp.concatenate([owned[:, :BLK], second], axis=1)
+        turn = turn_of(owned, high)
+        returned = turn_back(owned.reshape(count, deep, 2 * BLK), turn, low)
         return unpack_blocks(returned, matching[1][slots])
 
     return body

time: 264 us -> 253 us (0.958)
  the two profiles are of different devices: /device:TPU:25 before, /device:TPU:0 now
where the time goes in v5:
time: 253 us; the launch traced here: 250 us
  Pallas kernels  215 us (85%)
  waiting for transfers between devices  14.1 us (6%)
  matrix products  12.3 us (5%)
  local copies, waits for them, and re-layouts  6.68 us (3%)
    pallas_call x2, Pallas kernels, rotation_of(): pl.pallas_call(functools.partial(rotation_kernel, 2), out_shape=jax.Shape...  94.7 us
    pallas_call x2, Pallas kernels, summed(): pl.pallas_call(functools.partial(sum_kernel, peers), out_shape=jax.ShapeD...  61.1 us
    pallas_call x1, Pallas kernels, spread(): pl.pallas_call(functools.partial(spread_kernel, low), out_shape=jax.Shape...  28.2 us
    pallas_call x1, Pallas kernels, turn_back(): pl.pallas_call(functools.partial(return_kernel, low), out_shape=jax.Shape...  27.8 us
    ppermute x1, waiting for transfers between devices, body(): second = lax.ppermute(owned[:, BLK:], GROUP, ring)  14.1 us
    dot_general x2, matrix products, gram_of(): lax.dot_general(cols_here, cols_here, (((0,), (0,)), ((), ())), precision...  8.76 us
  transfers between devices with their start and end apart: 1, of which 1 were waited for; matrix products, arithmetic and copies ran while one was open for 0% of the time, Pallas kernels for 0%

profile of v5, /device:TPU:0, one launch (start us, length us, event | category | flops | bytes accessed | tf_op | source)
XLA Modules:
  0.0 249.9 jit_solution(5442554733957171685)
XLA Ops:
  0.0 0.8 slice_bitcast_fusion
  0.8 0.7 pad_clamp_fusion
  1.4 0.7 gather_fusion.1
  2.1 0.0 copy-start
  2.1 1.6 copy-done
  3.7 0.7 shard_map.55.packed
  4.4 28.2 %shard_map.56 = f32[8,128,512]{2,1,0:T(8,128)S(1)} custom-call(f32[8,128,512]{2,1,0:T(8,128)S(1)} %shard_map.55.packed), custom_call_target="tpu_custom_call" | custom-call | tf_op jit(solution)/shard_map/pallas_call | solution.py:289
  32.6 3.6 %convolution_bitcast_fusion.gram_ref = f32[512,512]{1,0:T(8,128)S(1)} fusion(f32[8,128,512]{2,1,0:T(8,128)S(1)} %shard_map.56), kind=kOutput, calls=%fused_computation.3 | convolution fusion | flops 3221225472 | bytes 3145728 | tf_op jit(solution)/shard_map/dot_general | solution.py:120
  36.2 29.7 %shard_map.57.gram_ref = f32[512,512]{1,0:T(8,128)S(1)} custom-call(f32[512,512]{1,0:T(8,128)S(1)} %convolution_bitcast_fusion.gram_ref), custom_call_target="tpu_custom_call" | custom-call | tf_op jit(solution)/shard_map/pallas_call | solution.py:185
  65.9 47.4 %shard_map.58 = f32[512,512]{1,0:T(8,128)S(1)} custom-call(f32[512,512]{1,0:T(8,128)S(1)} %shard_map.57.gram_ref), custom_call_target="tpu_custom_call" | custom-call | tf_op jit(solution)/shard_map/pallas_call | solution.py:106
  113.3 3.5 %fusion.2 = f32[1024,512]{0,1:T(8,128)S(1)} fusion(f32[1024,512]{1,0:T(8,128)S(1)} %bitcast.12, f32[512,512]{1,0:T(8,128)S(1)} %shard_map.58), kind=kOutput, calls=%fused_computation.9 | convolution fusion | flops 3221225472 | bytes 5242880 | tf_op jit(solution)/shard_map/dot_general | solution.py:62
  116.9 0.1 fusion.1
  117.0 0.1 collective-permute-start
  117.1 0.7 gather_fusion
  117.8 14.1 %collective-permute-done = f32[1024,256]{0,1:T(8,128)S(1)} collective-permute-done((f32[1024,256]{0,1:T(8,128)S(1)}, f32[1024,256]{0,1:T(8,128)S(1)}, u32[]{:S(2)}, u32[]{:S(2)}) %collective-permute-start) | collective-permute-done | bytes 1048608 | tf_op jit(solution)/shard_map/ppermute | solution.py:367
  131.9 0.0 copy-start.1
  131.9 1.0 copy-done.1
  132.9 1.5 pad_maximum_fusion
  134.3 1.9 copy.7
  136.3 5.1 %fusion.gram_ref = f32[512,512]{1,0:T(8,128)S(1)} fusion(f32[1024,256]{0,1:T(8,128)} %copy-done.1, f32[1024,256]{0,1:T(8,128)S(1)} %get-tuple-element.5), kind=kOutput, calls=%fused_computation.7 | convolution fusion | flops 3221749760 | bytes 3145728 | tf_op jit(solution)/shard_map/dot_general | solution.py:120
  141.4 31.4 %shard_map.59.gram_ref = f32[512,512]{1,0:T(8,128)S(1)} custom-call(f32[512,512]{1,0:T(8,128)S(1)} %fusion.gram_ref), custom_call_target="tpu_custom_call" | custom-call | tf_op jit(solution)/shard_map/pallas_call | solution.py:185
  172.8 47.3 %shard_map.60.turn_ref = f32[512,512]{1,0:T(8,128)S(1)} custom-call(f32[512,512]{1,0:T(8,128)S(1)} %shard_map.59.gram_ref), custom_call_target="tpu_custom_call" | custom-call | tf_op jit(solution)/shard_map/pallas_call | solution.py:106
  220.1 27.8 %shard_map.61.src_ref = f32[8,128,512]{2,1,0:T(8,128)S(1)} custom-call(f32[8,128,512]{2,1,0:T(8,128)S(1)} %bitcast.13, f32[512,512]{1,0:T(8,128)S(1)} %shard_map.60.turn_ref), custom_call_target="tpu_custom_call" | custom-call | tf_op jit(solution)/shard_map/pallas_call | solution.py:322
  247.9 2.0 shard_map.62
Async XLA Ops:
  2.1 1.6 copy-start
  117.0 14.9 %collective-permute-start = (f32[1024,256]{0,1:T(8,128)S(1)}, f32[1024,256]{0,1:T(8,128)S(1)}, u32[]{:S(2)}, u32[]{:S(2)}) collective-permute-start(f32[1024,256]{0,1:T(8,128)S(1)} %get-tuple-element.6), channel_id=1, source_target_pairs={{0,8},{8,24},{24,16},{16,17},{17,25},{25,9},{9,1},{1,0},{2,10},{10... | collective-permute-start | bytes 3145736 | tf_op jit(solution)/shard_map/ppermute | solution.py:367
  131.9 1.0 copy-start.1
